TPU v7x, 256 devices: a whole 4x4x8 slice. The times are simulated.
256 devices in a mesh: row: 16 (over y_lo, z), col: 16 (over x, y_hi, core).
Axes of the slice: x: 4, y: 4 (y_hi: 2, y_lo: 2; y = y_hi * 2 + y_lo), z: 8, core: 2. Of those that a mesh axis runs over, the one named last changes fastest.
Arguments:
- pair: bfloat16 [992, 992, 128], P('row', 'col'), may hold values from -6 to 6
- pair_mask: int32 [992, 992], P('row', 'col'), may hold values 0 or 1
- norm_in_gain: float32 [128], replicated, may hold values from 0.1 to 1.9
- proj_weight: bfloat16 [128, 512], replicated, may hold values from -0.5 to 0.5
- gate_weight: bfloat16 [128, 128], replicated, may hold values from -0.5 to 0.5
- norm_mid_gain: float32 [128], replicated, may hold values from 0.1 to 1.9
- out_weight: bfloat16 [128, 128], replicated, may hold values from -0.5 to 0.5
- norm_tr_gain: float32 [128], replicated, may hold values from 0.1 to 1.9
- tr_in_weight: bfloat16 [128, 1024], replicated, may hold values from -0.5 to 0.5
- tr_out_weight: bfloat16 [512, 128], replicated, may hold values from -0.25 to 0.25
Outputs:
- new_pair: bfloat16 [992, 992, 128], P('row', 'col')
All inputs are finite; a program needn't handle non-finite values. No bound on the sum of `pair_mask` on one device may be relied on, other than what follows from the above.
Results may differ from a plain program's by a relative error of at most 0.02.
Values may be sent and summed in bfloat16 or wider, within the bound.
No kernel may reach another device: no remote copies, remote signals or barrier semaphores. Data moves between devices by JAX's collectives and lax.ppermute only.
A program may use at most 192 MiB of HBM per device.

v0:
```python
import jax
import jax.numpy as jnp
from jax import lax
from jax.sharding import PartitionSpec as P


def layer_norm(values, norm_gain):
    average = jnp.mean(values, axis=-1, keepdims=True)
    centered = values - average
    variance = jnp.mean(centered * centered, axis=-1, keepdims=True)
    return centered * lax.rsqrt(variance + 1e-05) * norm_gain


def gated_half(normed, keep_mask, weight_part, hidden_width):
    projected = jnp.dot(normed, weight_part, preferred_element_type=jnp.float32)
    gated = keep_mask * jax.nn.sigmoid(projected[:, :hidden_width]) * projected[:, hidden_width:]
    return gated.astype(jnp.bfloat16)


def finish(
    pair_rows,
    normed,
    combined,
    gate_weight,
    norm_mid_gain,
    out_weight,
    norm_tr_gain,
    tr_in_weight,
    tr_out_weight,
):
    residual_in = pair_rows.astype(jnp.float32)
    gate_value = jax.nn.sigmoid(jnp.dot(normed, gate_weight, preferred_element_type=jnp.float32))
    mixed_norm = layer_norm(combined, norm_mid_gain).astype(jnp.bfloat16)
    update = gate_value * jnp.dot(mixed_norm, out_weight, preferred_element_type=jnp.float32)
    middle = lax.optimization_barrier((residual_in + update).astype(jnp.bfloat16))
    middle_wide = middle.astype(jnp.float32)
    tr_normed = layer_norm(middle_wide, norm_tr_gain).astype(jnp.bfloat16)
    tr_width = tr_out_weight.shape[0]
    hidden = jnp.dot(tr_normed, tr_in_weight, preferred_element_type=jnp.float32)
    activated = (jax.nn.silu(hidden[:, :tr_width]) * hidden[:, tr_width:]).astype(jnp.bfloat16)
    return (
        middle_wide + jnp.dot(activated, tr_out_weight, preferred_element_type=jnp.float32)
    ).astype(jnp.bfloat16)


def local(
    pair,
    pair_mask,
    norm_in_gain,
    proj_weight,
    gate_weight,
    norm_mid_gain,
    out_weight,
    norm_tr_gain,
    tr_in_weight,
    tr_out_weight,
):
    rows_here, cols_here, channels = pair.shape
    hidden_width = proj_weight.shape[1] // 4
    flat_pair = pair.reshape(rows_here * cols_here, channels)
    normed = layer_norm(flat_pair.astype(jnp.float32), norm_in_gain).astype(jnp.bfloat16)
    keep_mask = pair_mask.reshape(-1, 1).astype(jnp.float32)
    right_weight = proj_weight[:, 2 * hidden_width :]
    left_gated = gated_half(normed, keep_mask, proj_weight[:, : 2 * hidden_width], hidden_width)
    left_tile = left_gated.reshape(rows_here, cols_here, hidden_width)
    right_tile = gated_half(normed, keep_mask, right_weight, hidden_width).reshape(
        rows_here, cols_here, hidden_width
    )
    gathered_keys = lax.all_gather(right_tile, "row", axis=0, tiled=True)
    combined = lax.psum_scatter(
        jnp.einsum(
            "jkc,ikc->jic", gathered_keys, left_tile, preferred_element_type=jnp.float32
        ).astype(jnp.bfloat16),
        "col",
        scatter_dimension=0,
        tiled=True,
    ).astype(jnp.float32)
    combined_rows = jnp.transpose(combined, (1, 0, 2)).reshape(rows_here * cols_here, hidden_width)
    new_rows = finish(
        flat_pair,
        normed,
        combined_rows,
        gate_weight,
        norm_mid_gain,
        out_weight,
        norm_tr_gain,
        tr_in_weight,
        tr_out_weight,
    )
    return new_rows.reshape(rows_here, cols_here, channels)


def solution(mesh):
    in_specs = (P("row", "col", None), P("row", "col"), P(), P(), P(), P(), P(), P(), P(), P())
    out_specs = P("row", "col", None)
    return jax.shard_map(local, mesh=mesh, in_specs=in_specs, out_specs=out_specs, check_vma=False)
```

profile of v0, /device:TPU:2, one launch (start us, length us, event | category | flops | bytes accessed | tf_op | source)
XLA Modules:
  0.0 482.9 jit_solution(6678963175934820104)
XLA Ops:
  6.5 1.4 reshape.107
  8.1 0.6 convert_reduce_fusion.1
  8.7 1.2 multiply_reduce_fusion.1
  10.2 2.2 multiply_convert_fusion.1
  12.4 2.5 fusion.32
  14.9 2.6 fusion.34
  17.5 0.1 convert_element_type.61
  17.6 5.1 %fusion.13 = (bf16[3844,128]{1,0:T(8,128)(2,1)}, bf16[3844,128]{1,0:T(8,128)(2,1)}) fusion(f32[3844,256]{1,0:T(8,128)} %fusion.32, f32[3844]{0:T(1024)S(1)} %convert_element_type.61, f32[3844,256]{1,0:T(8,128)} %fusion.34), kind=kLoop, calls=%fused_computation.23 | loop fusion | flops 5904384 | bytes 9856016 | tf_op jit(solution)/shard_map/convert_element_type | solution.py:17
  22.7 2.2 reshape.104
  25.0 0.2 reduce-scatter.2.cloned.1.call-start
  25.2 2.2 reshape.103
  27.4 5.1 %copy.35 = bf16[62,62,128]{1,0,2:T(8,128)(2,1)} copy(bf16[62,62,128]{2,1,0:T(8,128)(2,1)} %reshape.103) | data formatting | bytes 1968128 | tf_op jit(solution)/shard_map/reshape | solution.py:65
  32.5 175.6 %all-gather.2.cloned.1.call-done = bf16[992,62,128]{2,1,0:T(8,128)(2,1)} async-done(((bf16[62,62,128]{2,1,0:T(8,128)(2,1)}), bf16[992,62,128]{2,1,0:T(8,128)(2,1)}) %all-gather.2.cloned.1.call-update) | async-done | bytes 15745040 | tf_op jit(solution)/shard_map/all_gather | solution.py:69
  208.1 49.8 %copy.36 = bf16[992,62,128]{1,0,2:T(8,128)(2,1)} copy(bf16[992,62,128]{2,1,0:T(8,128)(2,1)} %all-gather.2.cloned.1.call-done) | data formatting | bytes 31490048 | tf_op jit(solution)/shard_map/all_gather | solution.py:69
  257.9 21.6 %convert_bitcast_fusion = bf16[992,62,128]{0,1,2:T(8,128)(2,1)} fusion(bf16[62,62,128]{1,0,2:T(8,128)(2,1)} %copy.35, bf16[992,62,128]{1,0,2:T(8,128)(2,1)} %copy.36), kind=kOutput, calls=%fused_computation | convolution fusion | flops 984064000 | bytes 32474112 | tf_op jit(solution)/shard_map/jkc,ikc->jic/dot_general | solution.py:71
  279.5 25.9 %copy.37 = bf16[992,62,128]{2,1,0:T(8,128)(2,1)} copy(bf16[992,62,128]{0,1,2:T(8,128)(2,1)} %convert_bitcast_fusion) | data formatting | bytes 31490048 | tf_op jit(solution)/shard_map/convert_element_type | solution.py:73
  305.4 0.7 copy-done.10
  306.2 2.0 fusion.4
  308.1 148.1 %reduce-scatter.2.cloned.1.call-done = bf16[62,62,128]{2,1,0:T(8,128)(2,1)} async-done(((bf16[992,62,128]{2,1,0:T(8,128)(2,1)}), bf16[62,62,128]{2,1,0:T(8,128)(2,1)}) %reduce-scatter.2.cloned.1.call-update) | async-done | bytes 984080 | tf_op jit(solution)/shard_map/reduce_scatter | solution.py:70
  456.2 1.9 fusion.23
  458.3 0.1 div.42
  458.5 1.2 multiply_reduce_fusion
  459.8 0.1 rsqrt.33
  459.9 0.2 convert_bitcast_fusion.1
  460.1 2.5 copy.38
  462.6 2.6 reshape.105
  465.2 3.4 fusion.5
  468.6 0.3 convert_reduce_fusion
  469.0 1.1 fusion.10
  470.2 2.3 fusion.24
  472.4 2.4 fusion.6
  474.9 1.2 reshape.106
  (36 shorter events, 0.8 us)
Async XLA Ops:
  6.5 463.6 %copy-start = (bf16[128,1024]{1,0:T(8,128)(2,1)S(1)}, bf16[128,1024]{1,0:T(8,128)(2,1)}, u32[]{:S(2)}) copy-start(bf16[128,1024]{1,0:T(8,128)(2,1)} %param.18) | copy-start | bytes 786436
  6.5 1.6 copy-start.1
  6.5 3.6 copy-start.8
  6.5 201.5 %all-gather.2.cloned.1.call-start = ((), (), s32[]{:S(2)}) async-start(), calls=%async_computation.1 | async-start | bytes 17268736 | tf_op jit(solution)/shard_map/all_gather | solution.py:69
  8.7 3.7 copy-start.3
  14.9 2.6 copy-start.5
  25.0 431.3 %reduce-scatter.2.cloned.1.call-start = ((), (), s32[]{:S(2)}) async-start(), calls=%async_computation.2 | async-start | bytes 17268736 | tf_op jit(solution)/shard_map/reduce_scatter | solution.py:70
  305.4 0.8 copy-start.10
  456.2 2.2 copy-start.2
  462.6 2.6 copy-start.4
  462.6 2.6 copy-start.7
  468.6 1.5 copy-start.6
  470.1 2.3 copy-start.9
Sparse Core Ops, SparseCore 0:
  25.1 182.9 all-gather.1
  305.5 150.6 reduce-scatter.1
where the time goes:
time: 486 us; the launch traced here: 483 us
  waiting for transfers between devices  324 us (67%)
  local copies, waits for them, and re-layouts  94.7 us (19%)
  matrix products  36.7 us (8%)
  other arithmetic  13.9 us (3%)
  between operations  13.6 us (3%)
    all_gather x1, waiting for transfers between devices, local(): gathered_keys = lax.all_gather(right_tile, 'row', axis=0, tiled=True)  176 us
    reduce_scatter x1, waiting for transfers between devices, local(): lax.psum_scatter(jnp.einsum('jkc,ikc->jic', gathered_keys, left_tile, pre...  148 us
    all_gather x1, local copies, waits for them, and re-layouts, local(): gathered_keys = lax.all_gather(right_tile, 'row', axis=0, tiled=True)  49.8 us
    convert_element_type x1, local copies, waits for them, and re-layouts, local(): combined = lax.psum_scatter(jnp.einsum('jkc,ikc->jic', gathered_keys, lef...  25.9 us
    dot_general x1, matrix products, local(): jnp.einsum('jkc,ikc->jic', gathered_keys, left_tile, preferred_element_ty...  21.6 us
  transfers between devices with their start and end apart: 2, of which 2 were waited for; matrix products, arithmetic and copies ran while one was open for 2% of the time, Pallas kernels for 0%

commit v1 on v0

v1 whole, which is shorter than its diff:
```python
import functools

import jax
import jax.numpy as jnp
from jax import lax
from jax.experimental import pallas as pl
from jax.experimental.pallas import tpu as pltpu
from jax.sharding import Mesh
from jax.sharding import PartitionSpec as P

SIDE = 64
LINES = 32
LANES = 128
VMEM_LIMIT = 48 * 1024 * 1024
F32 = jnp.float32
BF16 = jnp.bfloat16


def norm_rows(values, gain):
    average = jnp.mean(values, axis=-1, keepdims=True)
    centered = values - average
    variance = jnp.mean(centered * centered, axis=-1, keepdims=True)
    return centered * lax.rsqrt(variance + 1e-05) * gain


def swap_halves(values):
    return pltpu.roll(values, LANES // 2, axis=1)


def low_half(rows):
    return lax.broadcasted_iota(jnp.int32, (rows, LANES), 1) < LANES // 2


def project_kernel(side, step, pair_ref, mask_ref, gain_ref, weight_ref, out_ref, rows, mask, weight, lines):
    channels = pair_ref.shape[-1]
    rows[...] = jnp.zeros_like(rows)
    mask[...] = jnp.zeros_like(mask)
    mask[0:side, 0:side] = mask_ref[...].astype(F32)
    mask[0:LINES, :] = jnp.where(low_half(LINES), mask[0:LINES, :], swap_halves(mask[LINES:, :]))
    weight[...] = weight_ref[...].astype(F32).T.astype(BF16)
    gain = gain_ref[...]

    def body(group, _):
        for u in range(step):
            line = group * step + u
            for half in range(2):
                i = line if half == 0 else jnp.minimum(LINES + line, side - 1)
                start = (2 * u + half) * SIDE
                rows[start : start + side, :] = norm_rows(pair_ref[i].astype(F32), gain)
        projected = lax.dot_general(
            weight[...], rows[...].astype(BF16), (((1,), (1,)), ((), ())), preferred_element_type=F32
        )
        for u in range(step):
            line = group * step + u
            part = projected[:, u * LANES : (u + 1) * LANES]
            keep = mask[pl.ds(line, 1), :]
            for which in range(2):
                at = 2 * which * channels
                gate, value = part[at : at + channels], part[at + channels : at + 2 * channels]
                lines[:, which * LINES + line, :] = keep * jax.nn.sigmoid(gate) * value
        return 0

    lax.fori_loop(0, LINES // step, body, 0)
    out_ref[...] = lines[...].astype(BF16)


def project(pair, pair_mask, gain, weight):
    side, _, channels = pair.shape
    step = 4
    return pl.pallas_call(
        functools.partial(project_kernel, side, step),
        out_shape=jax.ShapeDtypeStruct((channels, 2 * LINES, LANES), BF16),
        scratch_shapes=[
            pltpu.VMEM((step * LANES, channels), F32),
            pltpu.VMEM((SIDE, LANES), F32),
            pltpu.VMEM((weight.shape[1], channels), BF16),
            pltpu.VMEM((channels, 2 * LINES, LANES), F32),
        ],
        compiler_params=pltpu.CompilerParams(vmem_limit_bytes=VMEM_LIMIT),
    )(pair, pair_mask, gain.reshape(1, -1), weight)


def multiply_kernel(blocks, chips, core_ref, in_ref, keep_ref, give_ref, left, right, product):
    core = core_ref[0]
    pairs = chips // 2
    low = low_half(LINES)

    def arrange(r, _):
        for which, target in enumerate((left, right)):
            for m in range(pairs):
                first = in_ref[r * chips + 2 * m, which * LINES : (which + 1) * LINES, :].astype(F32)
                second = in_ref[r * chips + 2 * m + 1, which * LINES : (which + 1) * LINES, :].astype(F32)
                columns = slice(m * LANES, (m + 1) * LANES)
                target[pl.ds(r * SIDE, LINES), columns] = jnp.where(low, first, swap_halves(second)).astype(BF16)
                target[pl.ds(r * SIDE + LINES, LINES), columns] = jnp.where(
                    low, swap_halves(first), second
                ).astype(BF16)
        return 0

    lax.fori_loop(0, blocks, arrange, 0)
    width = product.shape[1]
    groups = blocks * SIDE // width
    per_group = width // LANES
    for group in range(groups):
        product[...] = lax.dot_general(
            left[...],
            right[group * width : (group + 1) * width, :],
            (((1,), (1,)), ((), ())),
            preferred_element_type=F32,
        )

        def deliver(r, _):
            for m in range(per_group):
                columns = slice(m * LANES, (m + 1) * LANES)
                first = product[pl.ds(r * SIDE, LINES), columns]
                second = product[pl.ds(r * SIDE + LINES, LINES), columns]
                even = jnp.where(low, first, swap_halves(second))
                odd = jnp.where(low, swap_halves(first), second)
                piece = r * chips + group * per_group + m
                keep_ref[piece] = jnp.where(core == 0, even, odd).astype(BF16)
                give_ref[piece] = jnp.where(core == 0, odd, even).astype(BF16)
            return 0

        lax.fori_loop(0, blocks, deliver, 0)


def multiply(received, core, blocks, chips):
    depth = chips * SIDE
    shape = jax.ShapeDtypeStruct((blocks * chips, LINES, LANES), BF16)
    return pl.pallas_call(
        functools.partial(multiply_kernel, blocks, chips),
        out_shape=(shape, shape),
        in_specs=[pl.BlockSpec(memory_space=pltpu.SMEM), pl.BlockSpec(memory_space=pltpu.VMEM)],
        scratch_shapes=[
            pltpu.VMEM((blocks * SIDE, depth), BF16),
            pltpu.VMEM((blocks * SIDE, depth), BF16),
            pltpu.VMEM((blocks * SIDE, 256), F32),
        ],
        compiler_params=pltpu.CompilerParams(vmem_limit_bytes=VMEM_LIMIT),
    )(core, received)


def finish_kernel(
    side,
    step,
    pair_ref,
    in_ref,
    norm_in_ref,
    gate_ref,
    norm_mid_ref,
    out_weight_ref,
    norm_tr_ref,
    tr_in_ref,
    tr_out_ref,
    out_ref,
    rows,
    lines,
    result,
):
    hidden_width = tr_out_ref.shape[0]
    rows[...] = jnp.zeros_like(rows)
    lines[...] = in_ref[...].astype(F32)

    def body(group, _):
        mixed = []
        for u in range(step):
            line = group * step + u
            for half in range(2):
                i = line if half == 0 else jnp.minimum(LINES + line, side - 1)
                start = (2 * u + half) * SIDE
                rows[start : start + side, :] = pair_ref[i].astype(F32)
            combined = lines[:, line, :]
            average = jnp.mean(combined, axis=0, keepdims=True)
            centered = combined - average
            variance = jnp.mean(centered * centered, axis=0, keepdims=True)
            mixed.append((centered * lax.rsqrt(variance + 1e-05)).T)
        mixed_norm = (jnp.concatenate(mixed, axis=0) * norm_mid_ref[...]).astype(BF16)
        residual = rows[...]
        normed = norm_rows(residual, norm_in_ref[...]).astype(BF16)
        gate = jax.nn.sigmoid(jnp.dot(normed, gate_ref[...], preferred_element_type=F32))
        update = gate * jnp.dot(mixed_norm, out_weight_ref[...], preferred_element_type=F32)
        middle = (residual + update).astype(BF16).astype(F32)
        tr_normed = norm_rows(middle, norm_tr_ref[...]).astype(BF16)
        hidden = jnp.dot(tr_normed, tr_in_ref[...], preferred_element_type=F32)
        activated = (jax.nn.silu(hidden[:, :hidden_width]) * hidden[:, hidden_width:]).astype(BF16)
        result[...] = middle + jnp.dot(activated, tr_out_ref[...], preferred_element_type=F32)
        for u in range(step):
            line = group * step + u
            start = 2 * u * SIDE
            out_ref[line] = result[start : start + side, :].astype(BF16)

            @pl.when(LINES + line < side)
            def _():
                out_ref[LINES + line] = result[start + SIDE : start + SIDE + side, :].astype(BF16)

        return 0

    lax.fori_loop(0, LINES // step, body, 0)


def finish(pair, received, norm_in_gain, gate_weight, norm_mid_gain, out_weight, norm_tr_gain, tr_in_weight, tr_out_weight):
    side, _, channels = pair.shape
    step = 4
    return pl.pallas_call(
        functools.partial(finish_kernel, side, step),
        out_shape=jax.ShapeDtypeStruct(pair.shape, BF16),
        scratch_shapes=[
            pltpu.VMEM((step * LANES, channels), F32),
            pltpu.VMEM(received.shape, F32),
            pltpu.VMEM((step * LANES, channels), F32),
        ],
        compiler_params=pltpu.CompilerParams(vmem_limit_bytes=VMEM_LIMIT),
    )(
        pair,
        received,
        norm_in_gain.reshape(1, -1),
        gate_weight,
        norm_mid_gain.reshape(1, -1),
        out_weight,
        norm_tr_gain.reshape(1, -1),
        tr_in_weight,
        tr_out_weight,
    )


def local(
    blocks,
    chips,
    pair,
    pair_mask,
    norm_in_gain,
    proj_weight,
    gate_weight,
    norm_mid_gain,
    out_weight,
    norm_tr_gain,
    tr_in_weight,
    tr_out_weight,
):
    every_chip = ("row", "chip")
    sent = project(pair, pair_mask, norm_in_gain, proj_weight)
    received = lax.all_to_all(sent, every_chip, 0, 0, tiled=True)
    core = lax.axis_index("core").astype(jnp.int32).reshape(1)
    keep, give = multiply(received, core, blocks, chips)
    other = lax.ppermute(give, "core", [(0, 1), (1, 0)])
    combined = (keep.astype(F32) + other.astype(F32)).astype(BF16)
    returned = lax.all_to_all(combined, every_chip, 0, 0, tiled=True)
    return finish(
        pair, returned, norm_in_gain, gate_weight, norm_mid_gain, out_weight, norm_tr_gain, tr_in_weight, tr_out_weight
    )


def solution(mesh):
    blocks, columns = mesh.devices.shape
    chips = columns // 2
    split = Mesh(mesh.devices.reshape(blocks, chips, 2), ("row", "chip", "core"))
    in_specs = (P("row", ("chip", "core"), None), P("row", ("chip", "core"))) + (P(),) * 8
    out_specs = P("row", ("chip", "core"), None)
    return jax.shard_map(
        functools.partial(local, blocks, chips), mesh=split, in_specs=in_specs, out_specs=out_specs, check_vma=False
    )
```

time: 486 us -> 143 us (0.29)
  waiting for transfers between devices: 324 us -> 55.6 us
  local copies, waits for them, and re-layouts: 94.7 us -> 4.89 us
  blocking collectives: 0 us -> 37.6 us
  matrix products: 36.7 us -> 0 us
  Pallas kernels: 0 us -> 28.4 us
  starting transfers between devices: 0.22 us -> 15.5 us
  other arithmetic: 13.9 us -> 0.28 us
  between operations: 13.6 us -> 0.14 us
    all_gather x1 -> x0, waiting for transfers between devices: 176 us -> none  [local(): gathered_keys = lax.all_gather(right_tile, 'row', axis=0, tiled=True)]
    reduce_scatter x1 -> x0, waiting for transfers between devices: 148 us -> none  [local(): lax.psum_scatter(jnp.einsum('jkc,ikc->jic', gathered_keys, left_tile, pre...]
    all_to_all x0 -> x1, waiting for transfers between devices: none -> 53 us  [local(): received = lax.all_to_all(sent, every_chip, 0, 0, tiled=True)]
    all_gather x1 -> x0, local copies, waits for them, and re-layouts: 49.8 us -> none  [local(): gathered_keys = lax.all_gather(right_tile, 'row', axis=0, tiled=True)]
    all_to_all x0 -> x1, blocking collectives: none -> 37.6 us  [local(): returned = lax.all_to_all(combined, every_chip, 0, 0, tiled=True)]
    dot_general x7 -> x0, matrix products: 36.7 us -> none  [the longest x1 21.6 us: local(): jnp.einsum('jkc,ikc->jic', gathered_keys, left_tile, preferred_element_ty...]
    pallas_call x0 -> x3, Pallas kernels: none -> 28.4 us  [the longest x1 12 us: finish(): pl.pallas_call(functools.partial(finish_kernel, side, step), out_shape=ja...]
    convert_element_type x3 -> x0, local copies, waits for them, and re-layouts: 27.5 us -> none  [the longest x1 25.9 us: local(): combined = lax.psum_scatter(jnp.einsum('jkc,ikc->jic', gathered_keys, lef...]
  transfers between devices with their start and end apart: 2 -> 2, of which waited for: 2 -> 2; matrix products, arithmetic and copies ran while one was open for 2% -> 0% of each run, Pallas kernels for 0% -> 0%
where the time goes in v1:
time: 143 us; the launch traced here: 142 us
  waiting for transfers between devices  55.6 us (39%)
  blocking collectives  37.6 us (26%)
  Pallas kernels  28.4 us (20%)
  starting transfers between devices  15.5 us (11%)
  local copies, waits for them, and re-layouts  4.89 us (3%)
    all_to_all x1, waiting for transfers between devices, local(): received = lax.all_to_all(sent, every_chip, 0, 0, tiled=True)  53 us
    all_to_all x1, blocking collectives, local(): returned = lax.all_to_all(combined, every_chip, 0, 0, tiled=True)  37.6 us
    all_to_all x1, starting transfers between devices, local(): received = lax.all_to_all(sent, every_chip, 0, 0, tiled=True)  15.4 us
    pallas_call x1, Pallas kernels, finish(): pl.pallas_call(functools.partial(finish_kernel, side, step), out_shape=ja...  12 us
    pallas_call x1, Pallas kernels, multiply(): pl.pallas_call(functools.partial(multiply_kernel, blocks, chips), out_sha...  9.7 us
    pallas_call x1, Pallas kernels, project(): pl.pallas_call(functools.partial(project_kernel, side, step), out_shape=j...  6.69 us
    unnamed x26, local copies, waits for them, and re-layouts  4.89 us
  transfers between devices with their start and end apart: 2, of which 2 were waited for; matrix products, arithmetic and copies ran while one was open for 0% of the time, Pallas kernels for 0%

profile of v1, /device:TPU:2, one launch (start us, length us, event | category | flops | bytes accessed | tf_op | source)
XLA Modules:
  0.0 142.4 jit_solution(3011888168051632771)
XLA Ops:
  0.0 1.2 copy-done.1
  1.2 0.0 copy-start.4
  1.2 0.9 copy-done.4
  2.1 0.0 copy-start.6
  2.1 0.8 copy-done.6
  2.9 0.0 copy-start.9
  2.9 0.7 copy-done.9
  3.5 6.7 %shard_map.100 = bf16[128,64,128]{2,1,0:T(8,128)(2,1)S(1)} custom-call(bf16[62,62,128]{2,1,0:T(8,128)(2,1)S(1)} %copy-done.1, s32[62,62]{1,0:T(8,128)S(1)} %copy-done.6, f32[1,128]{1,0:T(1,128)S(1)} %bitcast.4, bf16[128,512]{1,0:T(8,128)(2,1)S(1)} %copy-done.4), custom_call_target="tpu_custom_call" | custom-call | tf_op jit(solution)/shard_map/pallas_call | solution.py:70
  10.2 0.0 copy-start
  10.2 1.3 copy-done
  11.6 15.4 %all-to-all-start = ((bf16[128,64,128]{2,1,0:T(8,128)(2,1)}), bf16[128,64,128]{2,1,0:T(8,128)(2,1)S(1)}, u32[]{:S(2)}, u32[]{:S(2)}) async-start(bf16[128,64,128]{2,1,0:T(8,128)(2,1)} %copy-done), calls=%async_computation | async-start | bytes 4194304 | tf_op jit(solution)/shard_map/all_to_all | solution.py:242
  27.0 53.0 %all-to-all-done.in_ref = bf16[128,64,128]{2,1,0:T(8,128)(2,1)S(1)} async-done(((bf16[128,64,128]{2,1,0:T(8,128)(2,1)}), bf16[128,64,128]{2,1,0:T(8,128)(2,1)S(1)}, u32[]{:S(2)}, u32[]{:S(2)}) %all-to-all-start) | async-done | bytes 2097184 | tf_op jit(solution)/shard_map/all_to_all | solution.py:242
  80.0 9.7 %shard_map.101 = (bf16[128,32,128]{2,1,0:T(8,128)(2,1)S(1)}, bf16[128,32,128]{2,1,0:T(8,128)(2,1)S(1)}) custom-call(s32[1]{0:T(128)} %bitcast.core_ref, bf16[128,64,128]{2,1,0:T(8,128)(2,1)S(1)} %all-to-all-done.in_ref), custom_call_target="tpu_custom_call" | custom-call | tf_op jit(solution)/shard_map/pallas_call | solution.py:130
  89.7 0.1 collective-permute-start
  89.8 2.6 %collective-permute-done = bf16[128,32,128]{2,1,0:T(8,128)(2,1)S(1)} collective-permute-done((bf16[128,32,128]{2,1,0:T(8,128)(2,1)S(1)}, bf16[128,32,128]{2,1,0:T(8,128)(2,1)S(1)}, u32[]{:S(2)}, u32[]{:S(2)}) %collective-permute-start) | collective-permute-done | bytes 1048608 | tf_op jit(solution)/shard_map/ppermute | solution.py:245
  92.4 0.0 copy-start.2
  92.4 0.0 copy-start.3
  92.4 0.0 copy-start.8
  92.4 0.0 copy-start.10
  92.5 0.0 copy-start.11
  92.5 0.0 copy-start.12
  92.5 0.3 add_convert_fusion
  92.8 37.6 %all_to_all.10.in_ref = bf16[128,32,128]{2,1,0:T(8,128)(2,1)S(1)} all-to-all(bf16[128,32,128]{2,1,0:T(8,128)(2,1)S(1)} %add_convert_fusion), channel_id=1, replica_groups=mesh['row'=16,'chip'=8,'core'=2] {'row','chip'}, dimensions={0} | all-to-all | bytes 2097152 | tf_op jit(solution)/shard_map/all_to_all | solution.py:247
  130.4 0.0 copy-done.2
  130.4 0.0 copy-done.3
  130.4 0.0 copy-done.5
  130.4 0.0 copy-done.7
  130.4 0.0 copy-done.8
  130.4 0.0 copy-done.10
  130.4 0.0 copy-done.11
  130.4 0.0 copy-done.12
  130.4 12.0 %shard_map.102 = bf16[62,62,128]{2,1,0:T(8,128)(2,1)} custom-call(bf16[62,62,128]{2,1,0:T(8,128)(2,1)S(1)} %copy-done.2, bf16[128,32,128]{2,1,0:T(8,128)(2,1)S(1)} %all_to_all.10.in_ref, f32[1,128]{1,0:T(1,128)S(1)} %bitcast.5, bf16[128,128]{1,0:T(8,128)(2,1)S(1)} %copy-done.7, f32[1,128]{1,0:T(1,128)S(1)} %bitcast.6, bf16[128,128]{1,0:T(8,128)(2,1)S(1)} %copy-done.8, ...), custom_call_target="tpu_custom_call" | custom-call | tf_op jit(solution)/shard_map/pallas_call | solution.py:204
  (3 shorter events, 0.0 us)
Async XLA Ops:
  0.0 1.2 copy-start.1
  1.2 0.9 copy-start.4
  2.1 0.8 copy-start.6
  2.9 0.7 copy-start.9
  10.2 1.3 copy-start
  11.6 68.4 %all-to-all-start = ((bf16[128,64,128]{2,1,0:T(8,128)(2,1)}), bf16[128,64,128]{2,1,0:T(8,128)(2,1)S(1)}, u32[]{:S(2)}, u32[]{:S(2)}) async-start(bf16[128,64,128]{2,1,0:T(8,128)(2,1)} %copy-done), calls=%async_computation | async-start | bytes 4194304 | tf_op jit(solution)/shard_map/all_to_all | solution.py:242
  89.7 2.7 %collective-permute-start = (bf16[128,32,128]{2,1,0:T(8,128)(2,1)S(1)}, bf16[128,32,128]{2,1,0:T(8,128)(2,1)S(1)}, u32[]{:S(2)}, u32[]{:S(2)}) collective-permute-start(bf16[128,32,128]{2,1,0:T(8,128)(2,1)S(1)} %get-tuple-element.8), channel_id=1, source_target_pairs={{0,1},{1,0},{2,3},{3,2},{4,5},{5,4},{6,7},{7,6},{8,9},{9,8},{10,11... | collective-permute-start | bytes 3145736 | tf_op jit(solution)/shard_map/ppermute | solution.py:245
  92.4 37.9 %copy-start.2 = (bf16[62,62,128]{2,1,0:T(8,128)(2,1)S(1)}, bf16[62,62,128]{2,1,0:T(8,128)(2,1)}, u32[]{:S(2)}) copy-start(bf16[62,62,128]{2,1,0:T(8,128)(2,1)} %pair_ref.3) | copy-start | bytes 2952196
  92.4 37.9 %copy-start.3 = (bf16[128,1024]{1,0:T(8,128)(2,1)S(1)}, bf16[128,1024]{1,0:T(8,128)(2,1)}, u32[]{:S(2)}) copy-start(bf16[128,1024]{1,0:T(8,128)(2,1)} %tr_in_ref.1) | copy-start | bytes 786436
  92.4 37.9 %copy-start.5 = (bf16[512,128]{1,0:T(8,128)(2,1)S(1)}, bf16[512,128]{1,0:T(8,128)(2,1)}, u32[]{:S(2)}) copy-start(bf16[512,128]{1,0:T(8,128)(2,1)} %tr_out_ref.1) | copy-start | bytes 393220
  92.4 37.9 %copy-start.7 = (bf16[128,128]{1,0:T(8,128)(2,1)S(1)}, bf16[128,128]{1,0:T(8,128)(2,1)}, u32[]{:S(2)}) copy-start(bf16[128,128]{1,0:T(8,128)(2,1)} %gate_ref.1) | copy-start | bytes 98308
  92.4 38.0 %copy-start.8 = (bf16[128,128]{1,0:T(8,128)(2,1)S(1)}, bf16[128,128]{1,0:T(8,128)(2,1)}, u32[]{:S(2)}) copy-start(bf16[128,128]{1,0:T(8,128)(2,1)} %out_weight_ref.1) | copy-start | bytes 98308
  92.4 37.9 %copy-start.10 = (f32[128]{0:T(128)S(1)}, f32[128]{0:T(128)}, u32[]{:S(2)}) copy-start(f32[128]{0:T(128)} %param.12) | copy-start | bytes 1540
  92.5 37.9 %copy-start.11 = (f32[128]{0:T(128)S(1)}, f32[128]{0:T(128)}, u32[]{:S(2)}) copy-start(f32[128]{0:T(128)} %param.15) | copy-start | bytes 1540
  92.5 37.9 %copy-start.12 = (f32[128]{0:T(128)S(1)}, f32[128]{0:T(128)}, u32[]{:S(2)}) copy-start(f32[128]{0:T(128)} %param.17) | copy-start | bytes 1540

commit v2 on v1

v2 whole, which is shorter than its diff:
```python
import functools

import jax
import jax.numpy as jnp
from jax import lax
from jax.experimental import pallas as pl
from jax.experimental.pallas import tpu as pltpu
from jax.sharding import Mesh
from jax.sharding import PartitionSpec as P

SIDE = 64
LINES = 32
LANES = 128
VMEM_LIMIT = 48 * 1024 * 1024
F32 = jnp.float32
BF16 = jnp.bfloat16


def norm_rows(values, gain):
    channels = values.shape[-1]
    weight = jnp.full((channels, channels), 1.0 / channels, BF16)
    centered = values.astype(F32) - jnp.dot(values, weight, preferred_element_type=F32)
    variance = jnp.mean(centered * centered, axis=-1, keepdims=True)
    return (centered * lax.rsqrt(variance + 1e-05) * gain).astype(BF16)


def swap_halves(values):
    return pltpu.roll(values, LANES // 2, axis=1)


def low_half(rows):
    return lax.broadcasted_iota(jnp.int32, (rows, LANES), 1) < LANES // 2


def project_kernel(
    side,
    step,
    pair_hbm,
    mask_hbm,
    gain_hbm,
    weight_hbm,
    out_hbm,
    pair_ref,
    mask_ref,
    gain_ref,
    weight_ref,
    mask,
    rows,
    out_ref,
    sems,
    out_sems,
):
    channels = pair_ref.shape[-1]
    groups = LINES // step
    small = [
        pltpu.make_async_copy(source, target, sems.at[n])
        for n, (source, target) in enumerate(((mask_hbm, mask_ref), (weight_hbm, weight_ref), (gain_hbm, gain_ref)))
    ]
    parts = []
    for group in range(groups):
        for half in range(2):
            first = half * LINES + group * step
            span = pl.ds(first, min(step, side - first))
            parts.append(pltpu.make_async_copy(pair_hbm.at[span], pair_ref.at[span], sems.at[3 + len(parts)]))
    outgoing = []
    for copy in small + parts:
        copy.start()
    rows[...] = jnp.zeros_like(rows)
    mask[...] = jnp.zeros_like(mask)
    for copy in small:
        copy.wait()
    mask[0:side, 0:side] = mask_ref[...].astype(F32)
    low = low_half(LINES)
    keep = jnp.where(low, mask[0:LINES, :], swap_halves(mask[LINES:, :]))
    weight = weight_ref[...].astype(F32).T.astype(BF16)
    for group in range(groups):
        parts[2 * group].wait()
        parts[2 * group + 1].wait()
        for u in range(step):
            for half in range(2):
                i = half * LINES + group * step + u
                if i < side:
                    start = (2 * u + half) * SIDE
                    rows[start : start + side, :] = pair_ref[i]
        projected = lax.dot_general(
            weight, norm_rows(rows[...], gain_ref[...]), (((1,), (1,)), ((), ())), preferred_element_type=F32
        )
        for which in range(2):
            made = []
            for u in range(step):
                part = projected[:, u * LANES : (u + 1) * LANES]
                at = 2 * which * channels
                gate, value = part[at : at + channels], part[at + channels : at + 2 * channels]
                line = group * step + u
                made.append(keep[line : line + 1, :] * jax.nn.sigmoid(gate) * value)
            first = which * LINES + group * step
            span = pl.ds(first, step)
            out_ref[:, span, :] = pltpu.einshape("tcl->ctl", jnp.stack(made)).astype(BF16)
            copy = pltpu.make_async_copy(out_ref.at[:, span], out_hbm.at[:, span], out_sems.at[len(outgoing)])
            copy.start()
            outgoing.append(copy)
    for copy in outgoing:
        copy.wait()


def project(pair, pair_mask, gain, weight):
    side, _, channels = pair.shape
    step = 16
    return pl.pallas_call(
        functools.partial(project_kernel, side, step),
        out_shape=jax.ShapeDtypeStruct((channels, 2 * LINES, LANES), BF16),
        in_specs=[pl.BlockSpec(memory_space=pltpu.HBM)] * 4,
        out_specs=pl.BlockSpec(memory_space=pltpu.HBM),
        scratch_shapes=[
            pltpu.VMEM(pair.shape, BF16),
            pltpu.VMEM(pair_mask.shape, jnp.int32),
            pltpu.VMEM((1, channels), F32),
            pltpu.VMEM(weight.shape, BF16),
            pltpu.VMEM((SIDE, LANES), F32),
            pltpu.VMEM((step * LANES, channels), BF16),
            pltpu.VMEM((channels, 2 * LINES, LANES), BF16),
            pltpu.SemaphoreType.DMA((3 + 2 * LINES // step,)),
            pltpu.SemaphoreType.DMA((2 * LINES // step,)),
        ],
        compiler_params=pltpu.CompilerParams(vmem_limit_bytes=62 * 1024 * 1024),
    )(pair, pair_mask, gain.reshape(1, -1), weight)


def multiply_kernel(blocks, chips, parity_ref, in_ref, out_ref, left, right):
    parity = parity_ref[0]
    low = low_half(LINES)

    def arrange_left(r, _):
        for m in range(chips):
            left[pl.ds(r * LINES, LINES), m * LANES : (m + 1) * LANES] = in_ref[r * chips + m, 0:LINES, :]
        return 0

    def arrange_right(s, _):
        for m in range(chips):
            piece = in_ref[(2 * s + parity) * chips + m, LINES : 2 * LINES, :].astype(F32)
            swapped = swap_halves(piece)
            columns = slice(m * LANES, (m + 1) * LANES)
            for n, values in enumerate(
                (
                    jnp.where(low, piece, 0.0),
                    jnp.where(low, swapped, 0.0),
                    jnp.where(low, 0.0, swapped),
                    jnp.where(low, 0.0, piece),
                )
            ):
                right[pl.ds(s * LANES + n * LINES, LINES), columns] = values.astype(BF16)
        return 0

    lax.fori_loop(0, blocks, arrange_left, 0)
    lax.fori_loop(0, blocks // 2, arrange_right, 0)
    width = 2 * LANES
    for group in range(blocks // 4):
        product = lax.dot_general(
            left[...],
            right[group * width : (group + 1) * width, :],
            (((1,), (1,)), ((), ())),
            preferred_element_type=F32,
        ).astype(BF16)
        for r in range(blocks):
            for n in range(2):
                out_ref[r * chips + 2 * group + n] = product[
                    r * LINES : (r + 1) * LINES, n * LANES : (n + 1) * LANES
                ]


def multiply(received, parity, blocks, chips):
    return pl.pallas_call(
        functools.partial(multiply_kernel, blocks, chips),
        out_shape=jax.ShapeDtypeStruct((blocks * chips, LINES, LANES), BF16),
        in_specs=[pl.BlockSpec(memory_space=pltpu.SMEM), pl.BlockSpec(memory_space=pltpu.VMEM)],
        scratch_shapes=[
            pltpu.VMEM((blocks * LINES, chips * LANES), BF16),
            pltpu.VMEM((blocks // 2 * LANES, chips * LANES), BF16),
        ],
        compiler_params=pltpu.CompilerParams(vmem_limit_bytes=VMEM_LIMIT),
    )(parity, received)


def gate_kernel(side, pair_ref, gain_ref, gate_weight_ref, rows, gate):
    rows[...] = jnp.zeros_like(rows)
    for i in range(side):
        start = (2 * (i % LINES) + i // LINES) * SIDE
        rows[start : start + side, :] = pair_ref[i]
    normed = norm_rows(rows[...], gain_ref[...])
    gate[...] = jax.nn.sigmoid(jnp.dot(normed, gate_weight_ref[...], preferred_element_type=F32))


def gate_rows(pair, gain, gate_weight):
    side, _, channels = pair.shape
    return pl.pallas_call(
        functools.partial(gate_kernel, side),
        out_shape=(
            jax.ShapeDtypeStruct((LINES * LANES, channels), BF16),
            jax.ShapeDtypeStruct((LINES * LANES, channels), F32),
        ),
        compiler_params=pltpu.CompilerParams(vmem_limit_bytes=VMEM_LIMIT),
    )(pair, gain.reshape(1, -1), gate_weight)


def finish_kernel(
    side,
    step,
    rows_ref,
    gate_ref,
    in_ref,
    norm_mid_ref,
    out_weight_ref,
    norm_tr_ref,
    tr_in_ref,
    tr_out_ref,
    out_hbm,
    result,
    out_ref,
    sems,
):
    hidden_width = tr_out_ref.shape[0]
    outgoing = []
    for group in range(LINES // step):
        window = in_ref[:, group * step : (group + 1) * step, :].astype(F32)
        lines = pltpu.einshape("ctl->tcl", window)
        mixed = []
        for u in range(step):
            combined = lines[u]
            average = jnp.mean(combined, axis=0, keepdims=True)
            centered = combined - average
            variance = jnp.mean(centered * centered, axis=0, keepdims=True)
            mixed.append((centered * lax.rsqrt(variance + 1e-05)).T)
        mixed_norm = (jnp.concatenate(mixed, axis=0) * norm_mid_ref[...]).astype(BF16)
        span = slice(group * step * LANES, (group + 1) * step * LANES)
        update = gate_ref[span, :] * jnp.dot(mixed_norm, out_weight_ref[...], preferred_element_type=F32)
        middle = (rows_ref[span, :].astype(F32) + update).astype(BF16)
        tr_normed = norm_rows(middle, norm_tr_ref[...])
        hidden = jnp.dot(tr_normed, tr_in_ref[...], preferred_element_type=F32)
        activated = (jax.nn.silu(hidden[:, :hidden_width]) * hidden[:, hidden_width:]).astype(BF16)
        result[...] = middle.astype(F32) + jnp.dot(activated, tr_out_ref[...], preferred_element_type=F32)
        for half in range(2):
            first = half * LINES + group * step
            count = min(step, side - first)
            for u in range(count):
                start = (2 * u + half) * SIDE
                out_ref[first + u] = result[start : start + side, :].astype(BF16)
            copy = pltpu.make_async_copy(
                out_ref.at[pl.ds(first, count)], out_hbm.at[pl.ds(first, count)], sems.at[len(outgoing)]
            )
            copy.start()
            outgoing.append(copy)
    for copy in outgoing:
        copy.wait()


def finish(shape, rows, gate, received, norm_mid_gain, out_weight, norm_tr_gain, tr_in_weight, tr_out_weight):
    side, _, channels = shape
    step = 16
    return pl.pallas_call(
        functools.partial(finish_kernel, side, step),
        out_shape=jax.ShapeDtypeStruct(shape, BF16),
        out_specs=pl.BlockSpec(memory_space=pltpu.HBM),
        scratch_shapes=[
            pltpu.VMEM((step * LANES, channels), F32),
            pltpu.VMEM(shape, BF16),
            pltpu.SemaphoreType.DMA((2 * LINES // step,)),
        ],
        compiler_params=pltpu.CompilerParams(vmem_limit_bytes=VMEM_LIMIT),
    )(
        rows,
        gate,
        received,
        norm_mid_gain.reshape(1, -1),
        out_weight,
        norm_tr_gain.reshape(1, -1),
        tr_in_weight,
        tr_out_weight,
    )


def local(
    blocks,
    chips,
    pair,
    pair_mask,
    norm_in_gain,
    proj_weight,
    gate_weight,
    norm_mid_gain,
    out_weight,
    norm_tr_gain,
    tr_in_weight,
    tr_out_weight,
):
    every_chip = ("row", "chip")
    core = lax.axis_index("core").astype(jnp.int32).reshape(1)
    sent = project(pair, pair_mask, norm_in_gain, proj_weight)
    received = lax.all_to_all(sent, every_chip, 0, 0, tiled=True)
    rows, gate = gate_rows(pair, norm_in_gain, gate_weight)
    received, rows, gate = lax.optimization_barrier((received, rows, gate))
    other = lax.ppermute(multiply(received, 1 - core, blocks, chips), "core", [(0, 1), (1, 0)])
    keep = multiply(received, core, blocks, chips)
    combined = (keep.astype(F32) + other.astype(F32)).astype(BF16)
    returned = lax.all_to_all(combined, every_chip, 0, 0, tiled=True)
    return finish(
        pair.shape, rows, gate, returned, norm_mid_gain, out_weight, norm_tr_gain, tr_in_weight, tr_out_weight
    )


def solution(mesh):
    blocks, columns = mesh.devices.shape
    chips = columns // 2
    split = Mesh(mesh.devices.reshape(blocks, chips, 2), ("row", "chip", "core"))
    in_specs = (P("row", ("chip", "core"), None), P("row", ("chip", "core"))) + (P(),) * 8
    out_specs = P("row", ("chip", "core"), None)
    return jax.shard_map(
        functools.partial(local, blocks, chips), mesh=split, in_specs=in_specs, out_specs=out_specs, check_vma=False
    )
```

time: 143 us -> 123 us (0.86)
  Pallas kernels: 28.4 us -> 17.1 us
  waiting for transfers between devices: 55.6 us -> 49.4 us
  local copies, waits for them, and re-layouts: 4.89 us -> 2.36 us
    pallas_call x1, Pallas kernels: 12 us -> 6.03 us  [finish(): pl.pallas_call(functools.partial(finish_kernel, side, step), out_shape=ja...]
    pallas_call x1 -> x2, Pallas kernels: 9.7 us -> 5.09 us  [multiply(): pl.pallas_call(functools.partial(multiply_kernel, blocks, chips), out_sha...]
    all_to_all x1, waiting for transfers between devices: 53 us -> 49.4 us  [local(): received = lax.all_to_all(sent, every_chip, 0, 0, tiled=True)]
    ppermute x1, waiting for transfers between devices: 2.65 us -> 0.01 us  [local(): lax.ppermute(multiply(received, 1 - core, blocks, chips), 'core', [(0, 1)...]
    unnamed x26 -> x24, local copies, waits for them, and re-layouts: 4.89 us -> 2.36 us
    pallas_call x1, Pallas kernels: 6.69 us -> 4.79 us  [project(): pl.pallas_call(functools.partial(project_kernel, side, step), out_shape=j...]
  transfers between devices with their start and end apart: 2 -> 2, of which waited for: 2 -> 1; matrix products, arithmetic and copies ran while one was open for 0% -> 0% of each run, Pallas kernels for 0% -> 3%
where the time goes in v2:
time: 123 us
  waiting for transfers between devices  49.4 us (40%)
  blocking collectives  38 us (31%)
  Pallas kernels  17.1 us (14%)
  starting transfers between devices  15.7 us (13%)
  local copies, waits for them, and re-layouts  2.36 us (2%)
    all_to_all x1, waiting for transfers between devices, local(): received = lax.all_to_all(sent, every_chip, 0, 0, tiled=True)  49.4 us
    all_to_all x1, blocking collectives, local(): returned = lax.all_to_all(combined, every_chip, 0, 0, tiled=True)  38 us
    all_to_all x1, starting transfers between devices, local(): received = lax.all_to_all(sent, every_chip, 0, 0, tiled=True)  15.6 us
    pallas_call x1, Pallas kernels, finish(): pl.pallas_call(functools.partial(finish_kernel, side, step), out_shape=ja...  6.03 us
    pallas_call x2, Pallas kernels, multiply(): pl.pallas_call(functools.partial(multiply_kernel, blocks, chips), out_sha...  5.09 us
    pallas_call x1, Pallas kernels, project(): pl.pallas_call(functools.partial(project_kernel, side, step), out_shape=j...  4.79 us
  transfers between devices with their start and end apart: 2, of which 1 were waited for; matrix products, arithmetic and copies ran while one was open for 0% of the time, Pallas kernels for 3%

profile of v2, /device:TPU:2, one launch (start us, length us, event | category | flops | bytes accessed | tf_op | source)
XLA Modules:
  0.0 123.1 jit_solution(8398254359901684811)
XLA Ops:
  0.0 4.8 %shard_map.100 = bf16[128,64,128]{2,1,0:T(8,128)(2,1)} custom-call(bf16[62,62,128]{2,1,0:T(8,128)(2,1)} %pair_ref.1, s32[62,62]{1,0:T(8,128)} %mask_hbm.1, f32[1,128]{1,0:T(1,128)} %bitcast.4, bf16[128,512]{1,0:T(8,128)(2,1)} %weight_hbm.1), custom_call_target="tpu_custom_call" | custom-call | tf_op jit(solution)/shard_map/pallas_call | solution.py:109
  4.8 0.0 copy-start
  4.8 0.0 copy-start.8
  4.8 0.0 copy-start.9
  4.8 15.6 %all-to-all-start = ((bf16[128,64,128]{2,1,0:T(8,128)(2,1)}), bf16[128,64,128]{2,1,0:T(8,128)(2,1)S(1)}, u32[]{:S(2)}, u32[]{:S(2)}) async-start(bf16[128,64,128]{2,1,0:T(8,128)(2,1)} %shard_map.100), calls=%async_computation | async-start | bytes 4194304 | tf_op jit(solution)/shard_map/all_to_all | solution.py:298
  20.4 0.0 copy-done
  20.4 0.0 copy-done.8
  20.4 0.0 copy-done.9
  20.4 1.2 shard_map.101
  21.6 0.0 copy-start.1
  21.7 1.3 %copy-done.1 = f32[4096,128]{1,0:T(8,128)} copy-done((f32[4096,128]{1,0:T(8,128)}, f32[4096,128]{1,0:T(8,128)S(1)}, u32[]{:S(2)}) %copy-start.1) | copy-done | bytes 2097176
  23.0 1.0 copy-done.3
  24.0 49.4 %all-to-all-done.in_ref = bf16[128,64,128]{2,1,0:T(8,128)(2,1)S(1)} async-done(((bf16[128,64,128]{2,1,0:T(8,128)(2,1)}), bf16[128,64,128]{2,1,0:T(8,128)(2,1)S(1)}, u32[]{:S(2)}, u32[]{:S(2)}) %all-to-all-start) | async-done | bytes 2097184 | tf_op jit(solution)/shard_map/all_to_all | solution.py:298
  73.4 2.5 %shard_map.103 = bf16[128,32,128]{2,1,0:T(8,128)(2,1)S(1)} custom-call(s32[1]{0:T(128)S(6)} %sub.3.parity_ref, bf16[128,64,128]{2,1,0:T(8,128)(2,1)S(1)} %all-to-all-done.in_ref), custom_call_target="tpu_custom_call" | custom-call | tf_op jit(solution)/shard_map/pallas_call | solution.py:172
  75.9 0.1 collective-permute-start
  76.0 2.5 %shard_map.102 = bf16[128,32,128]{2,1,0:T(8,128)(2,1)S(1)} custom-call(s32[1]{0:T(128)} %bitcast.1.parity_ref, bf16[128,64,128]{2,1,0:T(8,128)(2,1)S(1)} %all-to-all-done.in_ref), custom_call_target="tpu_custom_call" | custom-call | tf_op jit(solution)/shard_map/pallas_call | solution.py:172
  78.6 0.0 copy-start.2
  78.6 0.0 copy-start.4
  78.6 0.0 copy-start.5
  78.6 0.0 copy-start.6
  78.6 0.0 copy-start.7
  78.6 0.0 copy-start.10
  78.6 0.0 copy-start.11
  78.7 0.0 collective-permute-done
  78.7 0.3 add_convert_fusion
  78.9 38.0 %all_to_all.10.in_ref = bf16[128,32,128]{2,1,0:T(8,128)(2,1)S(1)} all-to-all(bf16[128,32,128]{2,1,0:T(8,128)(2,1)S(1)} %add_convert_fusion), channel_id=1, replica_groups=mesh['row'=16,'chip'=8,'core'=2] {'row','chip'}, dimensions={0} | all-to-all | bytes 2097152 | tf_op jit(solution)/shard_map/all_to_all | solution.py:304
  116.9 0.0 copy-done.2
  116.9 0.0 copy-done.4
  116.9 0.0 copy-done.5
  116.9 0.0 copy-done.6
  116.9 0.0 copy-done.7
  117.0 6.0 %shard_map.104 = bf16[62,62,128]{2,1,0:T(8,128)(2,1)} custom-call(bf16[4096,128]{1,0:T(8,128)(2,1)S(1)} %copy-done.4, f32[4096,128]{1,0:T(8,128)S(1)} %copy-done.2, bf16[128,32,128]{2,1,0:T(8,128)(2,1)S(1)} %all_to_all.10.in_ref, f32[1,128]{1,0:T(1,128)S(1)} %bitcast.6, bf16[128,128]{1,0:T(8,128)(2,1)S(1)} %copy-done.7, f32[1,128]{1,0:T(1,128)S(1)} %bitcast.7, ...), custom_call_target="tpu_custom_call" | custom-call | tf_op jit(solution)/shard_map/pallas_call | solution.py:259
  (3 shorter events, 0.0 us)
Async XLA Ops:
  4.8 15.6 %copy-start = (bf16[62,62,128]{2,1,0:T(8,128)(2,1)S(1)}, bf16[62,62,128]{2,1,0:T(8,128)(2,1)}, u32[]{:S(2)}) copy-start(bf16[62,62,128]{2,1,0:T(8,128)(2,1)} %pair_ref.1) | copy-start | bytes 2952196
  4.8 15.6 %copy-start.8 = (bf16[128,128]{1,0:T(8,128)(2,1)S(1)}, bf16[128,128]{1,0:T(8,128)(2,1)}, u32[]{:S(2)}) copy-start(bf16[128,128]{1,0:T(8,128)(2,1)} %gate_weight_ref.1) | copy-start | bytes 98308
  4.8 15.6 %copy-start.9 = (f32[128]{0:T(128)S(1)}, f32[128]{0:T(128)}, u32[]{:S(2)}) copy-start(f32[128]{0:T(128)} %param.12) | copy-start | bytes 1540
  4.8 68.5 %all-to-all-start = ((bf16[128,64,128]{2,1,0:T(8,128)(2,1)}), bf16[128,64,128]{2,1,0:T(8,128)(2,1)S(1)}, u32[]{:S(2)}, u32[]{:S(2)}) async-start(bf16[128,64,128]{2,1,0:T(8,128)(2,1)} %shard_map.100), calls=%async_computation | async-start | bytes 4194304 | tf_op jit(solution)/shard_map/all_to_all | solution.py:298
  21.6 1.3 %copy-start.1 = (f32[4096,128]{1,0:T(8,128)}, f32[4096,128]{1,0:T(8,128)S(1)}, u32[]{:S(2)}) copy-start(f32[4096,128]{1,0:T(8,128)S(1)} %get-tuple-element.13.gate_ref) | copy-start | bytes 6291460
  23.0 1.0 copy-start.3
  75.9 2.7 %collective-permute-start = (bf16[128,32,128]{2,1,0:T(8,128)(2,1)S(1)}, bf16[128,32,128]{2,1,0:T(8,128)(2,1)S(1)}, u32[]{:S(2)}, u32[]{:S(2)}) collective-permute-start(bf16[128,32,128]{2,1,0:T(8,128)(2,1)S(1)} %shard_map.103), channel_id=1, source_target_pairs={{0,1},{1,0},{2,3},{3,2},{4,5},{5,4},{6,7},{7,6},{8,9},{9,8},{10,11... | collective-permute-start | bytes 3145736 | tf_op jit(solution)/shard_map/ppermute | solution.py:301
  78.6 38.3 %copy-start.2 = (f32[4096,128]{1,0:T(8,128)S(1)}, f32[4096,128]{1,0:T(8,128)}, u32[]{:S(2)}) copy-start(f32[4096,128]{1,0:T(8,128)} %copy-done.1) | copy-start | bytes 6291460
  78.6 38.3 %copy-start.4 = (bf16[4096,128]{1,0:T(8,128)(2,1)S(1)}, bf16[4096,128]{1,0:T(8,128)(2,1)}, u32[]{:S(2)}) copy-start(bf16[4096,128]{1,0:T(8,128)(2,1)} %copy-done.3) | copy-start | bytes 3145732
  78.6 38.3 %copy-start.5 = (bf16[128,1024]{1,0:T(8,128)(2,1)S(1)}, bf16[128,1024]{1,0:T(8,128)(2,1)}, u32[]{:S(2)}) copy-start(bf16[128,1024]{1,0:T(8,128)(2,1)} %tr_in_ref.1) | copy-start | bytes 786436
  78.6 38.3 %copy-start.6 = (bf16[512,128]{1,0:T(8,128)(2,1)S(1)}, bf16[512,128]{1,0:T(8,128)(2,1)}, u32[]{:S(2)}) copy-start(bf16[512,128]{1,0:T(8,128)(2,1)} %tr_out_ref.1) | copy-start | bytes 393220
  78.6 38.3 %copy-start.7 = (bf16[128,128]{1,0:T(8,128)(2,1)S(1)}, bf16[128,128]{1,0:T(8,128)(2,1)}, u32[]{:S(2)}) copy-start(bf16[128,128]{1,0:T(8,128)(2,1)} %out_weight_ref.1) | copy-start | bytes 98308
  78.6 38.3 %copy-start.10 = (f32[128]{0:T(128)S(1)}, f32[128]{0:T(128)}, u32[]{:S(2)}) copy-start(f32[128]{0:T(128)} %param.15) | copy-start | bytes 1540
  78.6 38.3 %copy-start.11 = (f32[128]{0:T(128)S(1)}, f32[128]{0:T(128)}, u32[]{:S(2)}) copy-start(f32[128]{0:T(128)} %param.17) | copy-start | bytes 1540

commit v3 on v2

--- a/solution.py
+++ b/solution.py
@@ -39,16 +39,14 @@
     mask_hbm,
     gain_hbm,
     weight_hbm,
-    out_hbm,
+    out_ref,
     pair_ref,
     mask_ref,
     gain_ref,
     weight_ref,
     mask,
     rows,
-    out_ref,
     sems,
-    out_sems,
 ):
     channels = pair_ref.shape[-1]
     groups = LINES // step
@@ -62,7 +60,6 @@
             first = half * LINES + group * step
             span = pl.ds(first, min(step, side - first))
             parts.append(pltpu.make_async_copy(pair_hbm.at[span], pair_ref.at[span], sems.at[3 + len(parts)]))
-    outgoing = []
     for copy in small + parts:
         copy.start()
     rows[...] = jnp.zeros_like(rows)
@@ -82,25 +79,23 @@
                 if i < side:
                     start = (2 * u + half) * SIDE
                     rows[start : start + side, :] = pair_ref[i]
-        projected = lax.dot_general(
-            weight, norm_rows(rows[...], gain_ref[...]), (((1,), (1,)), ((), ())), preferred_element_type=F32
-        )
+        sub = 16
+        made = ([], [])
+        for part in range(step // sub):
+            span = slice(part * sub * LANES, (part + 1) * sub * LANES)
+            projected = lax.dot_general(
+                weight, norm_rows(rows[span, :], gain_ref[...]), (((1,), (1,)), ((), ())), preferred_element_type=F32
+            )
+            for u in range(sub):
+                line = group * step + part * sub + u
+                cut = projected[:, u * LANES : (u + 1) * LANES]
+                for which in range(2):
+                    at = 2 * which * channels
+                    gate, value = cut[at : at + channels], cut[at + channels : at + 2 * channels]
+                    made[which].append(keep[line : line + 1, :] * jax.nn.sigmoid(gate) * value)
         for which in range(2):
-            made = []
-            for u in range(step):
-                part = projected[:, u * LANES : (u + 1) * LANES]
-                at = 2 * which * channels
-                gate, value = part[at : at + channels], part[at + channels : at + 2 * channels]
-                line = group * step + u
-                made.append(keep[line : line + 1, :] * jax.nn.sigmoid(gate) * value)
-            first = which * LINES + group * step
-            span = pl.ds(first, step)
-            out_ref[:, span, :] = pltpu.einshape("tcl->ctl", jnp.stack(made)).astype(BF16)
-            copy = pltpu.make_async_copy(out_ref.at[:, span], out_hbm.at[:, span], out_sems.at[len(outgoing)])
-            copy.start()
-            outgoing.append(copy)
-    for copy in outgoing:
-        copy.wait()
+            span = pl.ds(which * LINES + group * step, step)
+            out_ref[:, span, :] = pltpu.einshape("tcl->ctl", jnp.stack(made[which])).astype(BF16)
 
 
 def project(pair, pair_mask, gain, weight):
@@ -110,7 +105,6 @@
         functools.partial(project_kernel, side, step),
         out_shape=jax.ShapeDtypeStruct((channels, 2 * LINES, LANES), BF16),
         in_specs=[pl.BlockSpec(memory_space=pltpu.HBM)] * 4,
-        out_specs=pl.BlockSpec(memory_space=pltpu.HBM),
         scratch_shapes=[
             pltpu.VMEM(pair.shape, BF16),
             pltpu.VMEM(pair_mask.shape, jnp.int32),
@@ -118,43 +112,36 @@
             pltpu.VMEM(weight.shape, BF16),
             pltpu.VMEM((SIDE, LANES), F32),
             pltpu.VMEM((step * LANES, channels), BF16),
-            pltpu.VMEM((channels, 2 * LINES, LANES), BF16),
             pltpu.SemaphoreType.DMA((3 + 2 * LINES // step,)),
-            pltpu.SemaphoreType.DMA((2 * LINES // step,)),
         ],
-        compiler_params=pltpu.CompilerParams(vmem_limit_bytes=62 * 1024 * 1024),
-    )(pair, pair_mask, gain.reshape(1, -1), weight)
+        compiler_params=pltpu.CompilerParams(vmem_limit_bytes=VMEM_LIMIT),
+    )(*(pltpu.with_memory_space_constraint(x, pltpu.HBM) for x in (pair, pair_mask, gain.reshape(1, -1), weight)))
 
 
 def multiply_kernel(blocks, chips, parity_ref, in_ref, out_ref, left, right):
     parity = parity_ref[0]
     low = low_half(LINES)
 
-    def arrange_left(r, _):
+    for r in range(blocks):
         for m in range(chips):
-            left[pl.ds(r * LINES, LINES), m * LANES : (m + 1) * LANES] = in_ref[r * chips + m, 0:LINES, :]
-        return 0
-
-    def arrange_right(s, _):
-        for m in range(chips):
-            piece = in_ref[(2 * s + parity) * chips + m, LINES : 2 * LINES, :].astype(F32)
-            swapped = swap_halves(piece)
-            columns = slice(m * LANES, (m + 1) * LANES)
-            for n, values in enumerate(
-                (
-                    jnp.where(low, piece, 0.0),
-                    jnp.where(low, swapped, 0.0),
-                    jnp.where(low, 0.0, swapped),
-                    jnp.where(low, 0.0, piece),
-                )
-            ):
-                right[pl.ds(s * LANES + n * LINES, LINES), columns] = values.astype(BF16)
-        return 0
-
-    lax.fori_loop(0, blocks, arrange_left, 0)
-    lax.fori_loop(0, blocks // 2, arrange_right, 0)
+            left[r * LINES : (r + 1) * LINES, m * LANES : (m + 1) * LANES] = in_ref[r * chips + m, 0:LINES, :]
     width = 2 * LANES
     for group in range(blocks // 4):
+        for s in (2 * group, 2 * group + 1):
+            for m in range(chips):
+                piece = in_ref[(2 * s + parity) * chips + m, LINES : 2 * LINES, :].astype(F32)
+                swapped = swap_halves(piece)
+                columns = slice(m * LANES, (m + 1) * LANES)
+                for n, values in enumerate(
+                    (
+                        jnp.where(low, piece, 0.0),
+                        jnp.where(low, swapped, 0.0),
+                        jnp.where(low, 0.0, swapped),
+                        jnp.where(low, 0.0, piece),
+                    )
+                ):
+                    row = s * LANES + n * LINES
+                    right[row : row + LINES, columns] = values.astype(BF16)
         product = lax.dot_general(
             left[...],
             right[group * width : (group + 1) * width, :],
@@ -214,7 +201,6 @@
     tr_in_ref,
     tr_out_ref,
     out_hbm,
-    result,
     out_ref,
     sems,
 ):
@@ -223,32 +209,35 @@
     for group in range(LINES // step):
         window = in_ref[:, group * step : (group + 1) * step, :].astype(F32)
         lines = pltpu.einshape("ctl->tcl", window)
-        mixed = []
-        for u in range(step):
-            combined = lines[u]
-            average = jnp.mean(combined, axis=0, keepdims=True)
-            centered = combined - average
-            variance = jnp.mean(centered * centered, axis=0, keepdims=True)
-            mixed.append((centered * lax.rsqrt(variance + 1e-05)).T)
-        mixed_norm = (jnp.concatenate(mixed, axis=0) * norm_mid_ref[...]).astype(BF16)
-        span = slice(group * step * LANES, (group + 1) * step * LANES)
-        update = gate_ref[span, :] * jnp.dot(mixed_norm, out_weight_ref[...], preferred_element_type=F32)
-        middle = (rows_ref[span, :].astype(F32) + update).astype(BF16)
-        tr_normed = norm_rows(middle, norm_tr_ref[...])
-        hidden = jnp.dot(tr_normed, tr_in_ref[...], preferred_element_type=F32)
-        activated = (jax.nn.silu(hidden[:, :hidden_width]) * hidden[:, hidden_width:]).astype(BF16)
-        result[...] = middle.astype(F32) + jnp.dot(activated, tr_out_ref[...], preferred_element_type=F32)
-        for half in range(2):
-            first = half * LINES + group * step
-            count = min(step, side - first)
-            for u in range(count):
-                start = (2 * u + half) * SIDE
-                out_ref[first + u] = result[start : start + side, :].astype(BF16)
-            copy = pltpu.make_async_copy(
-                out_ref.at[pl.ds(first, count)], out_hbm.at[pl.ds(first, count)], sems.at[len(outgoing)]
-            )
-            copy.start()
-            outgoing.append(copy)
+        sub = 16
+        for part in range(step // sub):
+            mixed = []
+            for u in range(part * sub, (part + 1) * sub):
+                combined = lines[u]
+                average = jnp.mean(combined, axis=0, keepdims=True)
+                centered = combined - average
+                variance = jnp.mean(centered * centered, axis=0, keepdims=True)
+                mixed.append((centered * lax.rsqrt(variance + 1e-05)).T)
+            mixed_norm = (jnp.concatenate(mixed, axis=0) * norm_mid_ref[...]).astype(BF16)
+            begin = (group * step + part * sub) * LANES
+            span = slice(begin, begin + sub * LANES)
+            update = gate_ref[span, :] * jnp.dot(mixed_norm, out_weight_ref[...], preferred_element_type=F32)
+            middle = (rows_ref[span, :].astype(F32) + update).astype(BF16)
+            tr_normed = norm_rows(middle, norm_tr_ref[...])
+            hidden = jnp.dot(tr_normed, tr_in_ref[...], preferred_element_type=F32)
+            activated = (jax.nn.silu(hidden[:, :hidden_width]) * hidden[:, hidden_width:]).astype(BF16)
+            made = middle.astype(F32) + jnp.dot(activated, tr_out_ref[...], preferred_element_type=F32)
+            for half in range(2):
+                first = half * LINES + group * step + part * sub
+                count = min(sub, side - first)
+                for u in range(count):
+                    start = (2 * u + half) * SIDE
+                    out_ref[first + u] = made[start : start + side].astype(BF16)
+                copy = pltpu.make_async_copy(
+                    out_ref.at[pl.ds(first, count)], out_hbm.at[pl.ds(first, count)], sems.at[len(outgoing)]
+                )
+                copy.start()
+                outgoing.append(copy)
     for copy in outgoing:
         copy.wait()
 
@@ -261,9 +250,8 @@
         out_shape=jax.ShapeDtypeStruct(shape, BF16),
         out_specs=pl.BlockSpec(memory_space=pltpu.HBM),
         scratch_shapes=[
-            pltpu.VMEM((step * LANES, channels), F32),
             pltpu.VMEM(shape, BF16),
-            pltpu.SemaphoreType.DMA((2 * LINES // step,)),
+            pltpu.SemaphoreType.DMA((2 * LINES // 16,)),
         ],
         compiler_params=pltpu.CompilerParams(vmem_limit_bytes=VMEM_LIMIT),
     )(
@@ -295,12 +283,14 @@
     every_chip = ("row", "chip")
     core = lax.axis_index("core").astype(jnp.int32).reshape(1)
     sent = project(pair, pair_mask, norm_in_gain, proj_weight)
+    sent, core, twin = lax.optimization_barrier((sent, core, 1 - core))
     received = lax.all_to_all(sent, every_chip, 0, 0, tiled=True)
-    rows, gate = gate_rows(pair, norm_in_gain, gate_weight)
-    received, rows, gate = lax.optimization_barrier((received, rows, gate))
-    other = lax.ppermute(multiply(received, 1 - core, blocks, chips), "core", [(0, 1), (1, 0)])
+    received, late_pair = lax.optimization_barrier((received, pair))
+    other = lax.ppermute(multiply(received, twin, blocks, chips), "core", [(0, 1), (1, 0)])
     keep = multiply(received, core, blocks, chips)
+    rows, gate = gate_rows(late_pair, norm_in_gain, gate_weight)
     combined = (keep.astype(F32) + other.astype(F32)).astype(BF16)
+    combined, rows, gate = lax.optimization_barrier((combined, rows, gate))
     returned = lax.all_to_all(combined, every_chip, 0, 0, tiled=True)
     return finish(
         pair.shape, rows, gate, returned, norm_mid_gain, out_weight, norm_tr_gain, tr_in_weight, tr_out_weight

time: 123 us -> 121 us (0.984)
  blocking collectives: 38 us -> 106 us
  waiting for transfers between devices: 49.4 us -> 0.01 us
  starting transfers between devices: 15.7 us -> 0.09 us
  Pallas kernels: 17.1 us -> 14 us
  local copies, waits for them, and re-layouts: 2.36 us -> 0.05 us
    all_to_all x0 -> x1, blocking collectives: none -> 68.2 us  [local(): received = lax.all_to_all(sent, every_chip, 0, 0, tiled=True)]
    all_to_all x1 -> x0, waiting for transfers between devices: 49.4 us -> none  [local(): received = lax.all_to_all(sent, every_chip, 0, 0, tiled=True)]
    all_to_all x1 -> x0, starting transfers between devices: 15.6 us -> none  [local(): received = lax.all_to_all(sent, every_chip, 0, 0, tiled=True)]
    unnamed x24 -> x16, local copies, waits for them, and re-layouts: 2.36 us -> 0.05 us
    pallas_call x2, Pallas kernels: 5.09 us -> 2.87 us  [multiply(): pl.pallas_call(functools.partial(multiply_kernel, blocks, chips), out_sha...]
  transfers between devices with their start and end apart: 2 -> 1, of which waited for: 1 -> 0; matrix products, arithmetic and copies ran while one was open for 0% -> 0% of each run, Pallas kernels for 3% -> 2%
where the time goes in v3:
time: 121 us
  blocking collectives  106 us (88%)
  Pallas kernels  14 us (12%)
    all_to_all x1, blocking collectives, local(): received = lax.all_to_all(sent, every_chip, 0, 0, tiled=True)  68.2 us
    all_to_all x1, blocking collectives, local(): returned = lax.all_to_all(combined, every_chip, 0, 0, tiled=True)  37.8 us
    pallas_call x1, Pallas kernels, finish(): pl.pallas_call(functools.partial(finish_kernel, side, step), out_shape=ja...  6 us
    pallas_call x1, Pallas kernels, project(): pl.pallas_call(functools.partial(project_kernel, side, step), out_shape=j...  3.9 us
    pallas_call x2, Pallas kernels, multiply(): pl.pallas_call(functools.partial(multiply_kernel, blocks, chips), out_sha...  2.87 us
  transfers between devices with their start and end apart: 1, of which 0 were waited for; matrix products, arithmetic and copies ran while one was open for 0% of the time, Pallas kernels for 2%

profile of v3, /device:TPU:2, one launch (start us, length us, event | category | flops | bytes accessed | tf_op | source)
XLA Modules:
  0.0 120.7 jit_solution(5259446348144750368)
XLA Ops:
  0.0 3.9 %shard_map.100 = bf16[128,64,128]{2,1,0:T(8,128)(2,1)S(1)} custom-call(bf16[62,62,128]{2,1,0:T(8,128)(2,1)} %pair_ref, s32[62,62]{1,0:T(8,128)} %mask_hbm.1, f32[1,128]{1,0:T(1,128)} %bitcast.4, bf16[128,512]{1,0:T(8,128)(2,1)} %weight_hbm.1), custom_call_target="tpu_custom_call" | custom-call | tf_op jit(solution)/shard_map/pallas_call | solution.py:104
  3.9 68.2 %all_to_all.10.in_ref = bf16[128,64,128]{2,1,0:T(8,128)(2,1)S(1)} all-to-all(bf16[128,64,128]{2,1,0:T(8,128)(2,1)S(1)} %shard_map.100), channel_id=1, replica_groups=mesh['row'=16,'chip'=8,'core'=2] {'row','chip'}, dimensions={0} | all-to-all | bytes 4194304 | tf_op jit(solution)/shard_map/all_to_all | solution.py:287
  72.1 1.4 %shard_map.102 = bf16[128,32,128]{2,1,0:T(8,128)(2,1)S(1)} custom-call(s32[1]{0:T(128)S(6)} %sub.3.parity_ref, bf16[128,64,128]{2,1,0:T(8,128)(2,1)S(1)} %all_to_all.10.in_ref), custom_call_target="tpu_custom_call" | custom-call | tf_op jit(solution)/shard_map/pallas_call | solution.py:159
  73.5 0.0 copy-start
  73.6 0.0 copy-start.4
  73.6 0.0 copy-start.5
  73.6 0.1 collective-permute-start
  73.7 1.4 %shard_map.101 = bf16[128,32,128]{2,1,0:T(8,128)(2,1)S(1)} custom-call(s32[1]{0:T(128)} %bitcast.1.parity_ref, bf16[128,64,128]{2,1,0:T(8,128)(2,1)S(1)} %all_to_all.10.in_ref), custom_call_target="tpu_custom_call" | custom-call | tf_op jit(solution)/shard_map/pallas_call | solution.py:159
  75.1 0.0 copy-done
  75.1 0.0 copy-done.4
  75.1 0.0 copy-done.5
  75.2 1.2 shard_map.103
  76.4 0.0 copy-start.1
  76.4 0.0 copy-start.2
  76.4 0.0 copy-start.3
  76.4 0.0 copy-start.6
  76.4 0.0 copy-start.7
  76.4 0.0 collective-permute-done
  76.4 0.3 add_convert_fusion
  76.7 37.8 %all_to_all.11.in_ref = bf16[128,32,128]{2,1,0:T(8,128)(2,1)S(1)} all-to-all(bf16[128,32,128]{2,1,0:T(8,128)(2,1)S(1)} %add_convert_fusion), channel_id=1, replica_groups=mesh['row'=16,'chip'=8,'core'=2] {'row','chip'}, dimensions={0} | all-to-all | bytes 2097152 | tf_op jit(solution)/shard_map/all_to_all | solution.py:294
  114.5 0.0 copy-done.1
  114.5 0.0 copy-done.2
  114.5 0.0 copy-done.3
  114.5 0.0 copy-done.6
  114.6 0.0 copy-done.7
  114.6 6.0 %shard_map.104 = bf16[62,62,128]{2,1,0:T(8,128)(2,1)} custom-call(bf16[4096,128]{1,0:T(8,128)(2,1)S(1)} %get-tuple-element.22.rows_ref, f32[4096,128]{1,0:T(8,128)S(1)} %get-tuple-element.23.gate_ref, bf16[128,32,128]{2,1,0:T(8,128)(2,1)S(1)} %all_to_all.11.in_ref, f32[1,128]{1,0:T(1,128)S(1)} %bitcast.6, bf16[128,128]{1,0:T(8,128)(2,1)S(1)} %copy-done.3, ...), custom_call_target="tpu_custom_call" | custom-call | tf_op jit(solution)/shard_map/pallas_call | solution.py:248
Async XLA Ops:
  73.5 1.6 %copy-start = (bf16[62,62,128]{2,1,0:T(8,128)(2,1)S(1)}, bf16[62,62,128]{2,1,0:T(8,128)(2,1)}, u32[]{:S(2)}) copy-start(bf16[62,62,128]{2,1,0:T(8,128)(2,1)} %pair_ref) | copy-start | bytes 2952196
  73.6 1.6 %copy-start.4 = (bf16[128,128]{1,0:T(8,128)(2,1)S(1)}, bf16[128,128]{1,0:T(8,128)(2,1)}, u32[]{:S(2)}) copy-start(bf16[128,128]{1,0:T(8,128)(2,1)} %gate_weight_ref.1) | copy-start | bytes 98308
  73.6 1.6 %copy-start.5 = (f32[128]{0:T(128)S(1)}, f32[128]{0:T(128)}, u32[]{:S(2)}) copy-start(f32[128]{0:T(128)} %param.12) | copy-start | bytes 1540
  73.6 2.8 %collective-permute-start = (bf16[128,32,128]{2,1,0:T(8,128)(2,1)S(1)}, bf16[128,32,128]{2,1,0:T(8,128)(2,1)S(1)}, u32[]{:S(2)}, u32[]{:S(2)}) collective-permute-start(bf16[128,32,128]{2,1,0:T(8,128)(2,1)S(1)} %shard_map.102), channel_id=1, source_target_pairs={{0,1},{1,0},{2,3},{3,2},{4,5},{5,4},{6,7},{7,6},{8,9},{9,8},{10,11... | collective-permute-start | bytes 3145736 | tf_op jit(solution)/shard_map/ppermute | solution.py:289
  76.4 38.2 %copy-start.1 = (bf16[128,1024]{1,0:T(8,128)(2,1)S(1)}, bf16[128,1024]{1,0:T(8,128)(2,1)}, u32[]{:S(2)}) copy-start(bf16[128,1024]{1,0:T(8,128)(2,1)} %tr_in_ref.1) | copy-start | bytes 786436
  76.4 38.2 %copy-start.2 = (bf16[512,128]{1,0:T(8,128)(2,1)S(1)}, bf16[512,128]{1,0:T(8,128)(2,1)}, u32[]{:S(2)}) copy-start(bf16[512,128]{1,0:T(8,128)(2,1)} %tr_out_ref.1) | copy-start | bytes 393220
  76.4 38.2 %copy-start.3 = (bf16[128,128]{1,0:T(8,128)(2,1)S(1)}, bf16[128,128]{1,0:T(8,128)(2,1)}, u32[]{:S(2)}) copy-start(bf16[128,128]{1,0:T(8,128)(2,1)} %out_weight_ref.1) | copy-start | bytes 98308
  76.4 38.2 %copy-start.6 = (f32[128]{0:T(128)S(1)}, f32[128]{0:T(128)}, u32[]{:S(2)}) copy-start(f32[128]{0:T(128)} %param.15) | copy-start | bytes 1540
  76.4 38.2 %copy-start.7 = (f32[128]{0:T(128)S(1)}, f32[128]{0:T(128)}, u32[]{:S(2)}) copy-start(f32[128]{0:T(128)} %param.17) | copy-start | bytes 1540

commit v4 on v3

--- a/solution.py
+++ b/solution.py
@@ -177,16 +177,27 @@
     gate[...] = jax.nn.sigmoid(jnp.dot(normed, gate_weight_ref[...], preferred_element_type=F32))
 
 
-def gate_rows(pair, gain, gate_weight):
+def keep_kernel(blocks, chips, side, parity_ref, in_ref, pair_ref, gain_ref, gate_ref, out_ref, rows, gate, left, right):
+    gate_kernel(side, pair_ref, gain_ref, gate_ref, rows, gate)
+    multiply_kernel(blocks, chips, parity_ref, in_ref, out_ref, left, right)
+
+
+def multiply_and_gate(received, parity, blocks, chips, pair, gain, gate_weight):
     side, _, channels = pair.shape
     return pl.pallas_call(
-        functools.partial(gate_kernel, side),
+        functools.partial(keep_kernel, blocks, chips, side),
         out_shape=(
+            jax.ShapeDtypeStruct((blocks * chips, LINES, LANES), BF16),
             jax.ShapeDtypeStruct((LINES * LANES, channels), BF16),
             jax.ShapeDtypeStruct((LINES * LANES, channels), F32),
         ),
-        compiler_params=pltpu.CompilerParams(vmem_limit_bytes=VMEM_LIMIT),
-    )(pair, gain.reshape(1, -1), gate_weight)
+        in_specs=[pl.BlockSpec(memory_space=pltpu.SMEM)] + [pl.BlockSpec(memory_space=pltpu.VMEM)] * 4,
+        scratch_shapes=[
+            pltpu.VMEM((blocks * LINES, chips * LANES), BF16),
+            pltpu.VMEM((blocks // 2 * LANES, chips * LANES), BF16),
+        ],
+        compiler_params=pltpu.CompilerParams(vmem_limit_bytes=VMEM_LIMIT // 2),
+    )(parity, received, pair, gain.reshape(1, -1), gate_weight)
 
 
 def finish_kernel(
@@ -285,10 +296,8 @@
     sent = project(pair, pair_mask, norm_in_gain, proj_weight)
     sent, core, twin = lax.optimization_barrier((sent, core, 1 - core))
     received = lax.all_to_all(sent, every_chip, 0, 0, tiled=True)
-    received, late_pair = lax.optimization_barrier((received, pair))
     other = lax.ppermute(multiply(received, twin, blocks, chips), "core", [(0, 1), (1, 0)])
-    keep = multiply(received, core, blocks, chips)
-    rows, gate = gate_rows(late_pair, norm_in_gain, gate_weight)
+    keep, rows, gate = multiply_and_gate(received, core, blocks, chips, pair, norm_in_gain, gate_weight)
     combined = (keep.astype(F32) + other.astype(F32)).astype(BF16)
     combined, rows, gate = lax.optimization_barrier((combined, rows, gate))
     returned = lax.all_to_all(combined, every_chip, 0, 0, tiled=True)

time: 121 us -> 121 us (level)
    pallas_call x2 -> x1, Pallas kernels: 2.87 us -> 1.39 us  [multiply(): pl.pallas_call(functools.partial(multiply_kernel, blocks, chips), out_sha...]
    pallas_call x1, Pallas kernels: 1.2 us -> 2.44 us  [multiply_and_gate(): pl.pallas_call(functools.partial(keep_kernel, blocks, chips, side), out_s...]
  transfers between devices with their start and end apart: 1 -> 1, of which waited for: 0 -> 1; matrix products, arithmetic and copies ran while one was open for 0% -> 0% of each run, Pallas kernels for 2% -> 2%
where the time goes in v4:
time: 121 us; the launch traced here: 120 us
  blocking collectives  106 us (88%)
  Pallas kernels  13.7 us (11%)
    all_to_all x1, blocking collectives, local(): received = lax.all_to_all(sent, every_chip, 0, 0, tiled=True)  68.2 us
    all_to_all x1, blocking collectives, local(): returned = lax.all_to_all(combined, every_chip, 0, 0, tiled=True)  37.7 us
    pallas_call x1, Pallas kernels, finish(): pl.pallas_call(functools.partial(finish_kernel, side, step), out_shape=ja...  6 us
    pallas_call x1, Pallas kernels, project(): pl.pallas_call(functools.partial(project_kernel, side, step), out_shape=j...  3.9 us
    pallas_call x1, Pallas kernels, multiply_and_gate(): pl.pallas_call(functools.partial(keep_kernel, blocks, chips, side), out_s...  2.44 us
  transfers between devices with their start and end apart: 1, of which 1 were waited for; matrix products, arithmetic and copies ran while one was open for 0% of the time, Pallas kernels for 2%

profile of v4, /device:TPU:2, one launch (start us, length us, event | category | flops | bytes accessed | tf_op | source)
XLA Modules:
  0.0 120.4 jit_solution(17994615663333035735)
XLA Ops:
  0.0 3.9 %shard_map.100 = bf16[128,64,128]{2,1,0:T(8,128)(2,1)S(1)} custom-call(bf16[62,62,128]{2,1,0:T(8,128)(2,1)} %pair_ref.1, s32[62,62]{1,0:T(8,128)} %mask_hbm.1, f32[1,128]{1,0:T(1,128)} %bitcast.4, bf16[128,512]{1,0:T(8,128)(2,1)} %weight_hbm.1), custom_call_target="tpu_custom_call" | custom-call | tf_op jit(solution)/shard_map/pallas_call | solution.py:104
  3.9 68.2 %all_to_all.10.in_ref = bf16[128,64,128]{2,1,0:T(8,128)(2,1)S(1)} all-to-all(bf16[128,64,128]{2,1,0:T(8,128)(2,1)S(1)} %shard_map.100), channel_id=1, replica_groups=mesh['row'=16,'chip'=8,'core'=2] {'row','chip'}, dimensions={0} | all-to-all | bytes 4194304 | tf_op jit(solution)/shard_map/all_to_all | solution.py:298
  72.1 0.0 copy-start
  72.1 0.0 copy-start.3
  72.1 0.0 copy-start.5
  72.1 1.4 %shard_map.102 = bf16[128,32,128]{2,1,0:T(8,128)(2,1)S(1)} custom-call(s32[1]{0:T(128)S(6)} %sub.3.parity_ref, bf16[128,64,128]{2,1,0:T(8,128)(2,1)S(1)} %all_to_all.10.in_ref), custom_call_target="tpu_custom_call" | custom-call | tf_op jit(solution)/shard_map/pallas_call | solution.py:159
  73.5 0.1 collective-permute-start
  73.6 0.0 copy-done
  73.6 0.0 copy-done.3
  73.6 0.0 copy-done.5
  73.6 2.4 %shard_map.101 = (bf16[128,32,128]{2,1,0:T(8,128)(2,1)S(1)}, bf16[4096,128]{1,0:T(8,128)(2,1)S(1)}, f32[4096,128]{1,0:T(8,128)S(1)}) custom-call(s32[1]{0:T(128)} %bitcast.1.parity_ref, bf16[128,64,128]{2,1,0:T(8,128)(2,1)S(1)} %all_to_all.10.in_ref, bf16[62,62,128]{2,1,0:T(8,128)(2,1)S(1)} %copy-done, f32[1,128]{1,0:T(1,128)S(1)} %bitcast.5, ...), custom_call_target="tpu_custom_call" | custom-call | tf_op jit(solution)/shard_map/pallas_call | solution.py:187
  76.1 0.2 collective-permute-done
  76.2 0.0 copy-start.1
  76.2 0.0 copy-start.2
  76.3 0.0 copy-start.4
  76.3 0.0 copy-start.6
  76.3 0.0 copy-start.7
  76.3 0.3 add_convert_fusion
  76.6 37.7 %all_to_all.11.in_ref = bf16[128,32,128]{2,1,0:T(8,128)(2,1)S(1)} all-to-all(bf16[128,32,128]{2,1,0:T(8,128)(2,1)S(1)} %add_convert_fusion), channel_id=1, replica_groups=mesh['row'=16,'chip'=8,'core'=2] {'row','chip'}, dimensions={0} | all-to-all | bytes 2097152 | tf_op jit(solution)/shard_map/all_to_all | solution.py:303
  114.2 0.0 copy-done.1
  114.2 0.0 copy-done.2
  114.2 0.0 copy-done.4
  114.2 0.0 copy-done.6
  114.3 0.0 copy-done.7
  114.3 6.0 %shard_map.103 = bf16[62,62,128]{2,1,0:T(8,128)(2,1)} custom-call(bf16[4096,128]{1,0:T(8,128)(2,1)S(1)} %get-tuple-element.20.rows_ref, f32[4096,128]{1,0:T(8,128)S(1)} %get-tuple-element.21.gate_ref, bf16[128,32,128]{2,1,0:T(8,128)(2,1)S(1)} %all_to_all.11.in_ref, f32[1,128]{1,0:T(1,128)S(1)} %bitcast.6, bf16[128,128]{1,0:T(8,128)(2,1)S(1)} %copy-done.4, ...), custom_call_target="tpu_custom_call" | custom-call | tf_op jit(solution)/shard_map/pallas_call | solution.py:259
Async XLA Ops:
  72.1 1.5 %copy-start = (bf16[62,62,128]{2,1,0:T(8,128)(2,1)S(1)}, bf16[62,62,128]{2,1,0:T(8,128)(2,1)}, u32[]{:S(2)}) copy-start(bf16[62,62,128]{2,1,0:T(8,128)(2,1)} %pair_ref.1) | copy-start | bytes 2952196
  72.1 1.5 %copy-start.3 = (bf16[128,128]{1,0:T(8,128)(2,1)S(1)}, bf16[128,128]{1,0:T(8,128)(2,1)}, u32[]{:S(2)}) copy-start(bf16[128,128]{1,0:T(8,128)(2,1)} %gate_ref.1) | copy-start | bytes 98308
  72.1 1.5 %copy-start.5 = (f32[128]{0:T(128)S(1)}, f32[128]{0:T(128)}, u32[]{:S(2)}) copy-start(f32[128]{0:T(128)} %param.12) | copy-start | bytes 1540
  73.5 2.7 %collective-permute-start = (bf16[128,32,128]{2,1,0:T(8,128)(2,1)S(1)}, bf16[128,32,128]{2,1,0:T(8,128)(2,1)S(1)}, u32[]{:S(2)}, u32[]{:S(2)}) collective-permute-start(bf16[128,32,128]{2,1,0:T(8,128)(2,1)S(1)} %shard_map.102), channel_id=1, source_target_pairs={{0,1},{1,0},{2,3},{3,2},{4,5},{5,4},{6,7},{7,6},{8,9},{9,8},{10,11... | collective-permute-start | bytes 3145736 | tf_op jit(solution)/shard_map/ppermute | solution.py:299
  76.2 38.0 %copy-start.1 = (bf16[128,1024]{1,0:T(8,128)(2,1)S(1)}, bf16[128,1024]{1,0:T(8,128)(2,1)}, u32[]{:S(2)}) copy-start(bf16[128,1024]{1,0:T(8,128)(2,1)} %tr_in_ref.1) | copy-start | bytes 786436
  76.2 38.0 %copy-start.2 = (bf16[512,128]{1,0:T(8,128)(2,1)S(1)}, bf16[512,128]{1,0:T(8,128)(2,1)}, u32[]{:S(2)}) copy-start(bf16[512,128]{1,0:T(8,128)(2,1)} %tr_out_ref.1) | copy-start | bytes 393220
  76.3 38.0 %copy-start.4 = (bf16[128,128]{1,0:T(8,128)(2,1)S(1)}, bf16[128,128]{1,0:T(8,128)(2,1)}, u32[]{:S(2)}) copy-start(bf16[128,128]{1,0:T(8,128)(2,1)} %out_weight_ref.1) | copy-start | bytes 98308
  76.3 38.0 %copy-start.6 = (f32[128]{0:T(128)S(1)}, f32[128]{0:T(128)}, u32[]{:S(2)}) copy-start(f32[128]{0:T(128)} %param.15) | copy-start | bytes 1540
  76.3 38.0 %copy-start.7 = (f32[128]{0:T(128)S(1)}, f32[128]{0:T(128)}, u32[]{:S(2)}) copy-start(f32[128]{0:T(128)} %param.17) | copy-start | bytes 1540

commit v5 on v4

--- a/solution.py
+++ b/solution.py
@@ -217,38 +217,39 @@
 ):
     hidden_width = tr_out_ref.shape[0]
     outgoing = []
+    lines = []
     for group in range(LINES // step):
         window = in_ref[:, group * step : (group + 1) * step, :].astype(F32)
-        lines = pltpu.einshape("ctl->tcl", window)
-        sub = 16
-        for part in range(step // sub):
-            mixed = []
-            for u in range(part * sub, (part + 1) * sub):
-                combined = lines[u]
-                average = jnp.mean(combined, axis=0, keepdims=True)
-                centered = combined - average
-                variance = jnp.mean(centered * centered, axis=0, keepdims=True)
-                mixed.append((centered * lax.rsqrt(variance + 1e-05)).T)
-            mixed_norm = (jnp.concatenate(mixed, axis=0) * norm_mid_ref[...]).astype(BF16)
-            begin = (group * step + part * sub) * LANES
-            span = slice(begin, begin + sub * LANES)
-            update = gate_ref[span, :] * jnp.dot(mixed_norm, out_weight_ref[...], preferred_element_type=F32)
-            middle = (rows_ref[span, :].astype(F32) + update).astype(BF16)
-            tr_normed = norm_rows(middle, norm_tr_ref[...])
-            hidden = jnp.dot(tr_normed, tr_in_ref[...], preferred_element_type=F32)
-            activated = (jax.nn.silu(hidden[:, :hidden_width]) * hidden[:, hidden_width:]).astype(BF16)
-            made = middle.astype(F32) + jnp.dot(activated, tr_out_ref[...], preferred_element_type=F32)
-            for half in range(2):
-                first = half * LINES + group * step + part * sub
-                count = min(sub, side - first)
-                for u in range(count):
-                    start = (2 * u + half) * SIDE
-                    out_ref[first + u] = made[start : start + side].astype(BF16)
-                copy = pltpu.make_async_copy(
-                    out_ref.at[pl.ds(first, count)], out_hbm.at[pl.ds(first, count)], sems.at[len(outgoing)]
-                )
-                copy.start()
-                outgoing.append(copy)
+        block = pltpu.einshape("ctl->tcl", window)
+        lines += [block[u] for u in range(step)]
+    begin = 0
+    for count_lines in (24, 8):
+        mixed = []
+        for combined in lines[begin : begin + count_lines]:
+            average = jnp.mean(combined, axis=0, keepdims=True)
+            centered = combined - average
+            variance = jnp.mean(centered * centered, axis=0, keepdims=True)
+            mixed.append((centered * lax.rsqrt(variance + 1e-05)).T)
+        mixed_norm = (jnp.concatenate(mixed, axis=0) * norm_mid_ref[...]).astype(BF16)
+        span = slice(begin * LANES, (begin + count_lines) * LANES)
+        update = gate_ref[span, :] * jnp.dot(mixed_norm, out_weight_ref[...], preferred_element_type=F32)
+        middle = (rows_ref[span, :].astype(F32) + update).astype(BF16)
+        tr_normed = norm_rows(middle, norm_tr_ref[...])
+        hidden = jnp.dot(tr_normed, tr_in_ref[...], preferred_element_type=F32)
+        activated = (jax.nn.silu(hidden[:, :hidden_width]) * hidden[:, hidden_width:]).astype(BF16)
+        made = middle.astype(F32) + jnp.dot(activated, tr_out_ref[...], preferred_element_type=F32)
+        for half in range(2):
+            first = half * LINES + begin
+            count = min(count_lines, side - first)
+            for u in range(count):
+                start = (2 * u + half) * SIDE
+                out_ref[first + u] = made[start : start + side].astype(BF16)
+            copy = pltpu.make_async_copy(
+                out_ref.at[pl.ds(first, count)], out_hbm.at[pl.ds(first, count)], sems.at[len(outgoing)]
+            )
+            copy.start()
+            outgoing.append(copy)
+        begin += count_lines
     for copy in outgoing:
         copy.wait()
 

time: 121 us -> 121 us (level)
  no operation moved by 1% of the time
where the time goes in v5:
time: 121 us; the launch traced here: 120 us
  blocking collectives  106 us (88%)
  Pallas kernels  13.7 us (11%)
    all_to_all x1, blocking collectives, local(): received = lax.all_to_all(sent, every_chip, 0, 0, tiled=True)  68.2 us
    all_to_all x1, blocking collectives, local(): returned = lax.all_to_all(combined, every_chip, 0, 0, tiled=True)  37.7 us
    pallas_call x1, Pallas kernels, finish(): pl.pallas_call(functools.partial(finish_kernel, side, step), out_shape=ja...  6.02 us
    pallas_call x1, Pallas kernels, project(): pl.pallas_call(functools.partial(project_kernel, side, step), out_shape=j...  3.9 us
    pallas_call x1, Pallas kernels, multiply_and_gate(): pl.pallas_call(functools.partial(keep_kernel, blocks, chips, side), out_s...  2.44 us
  transfers between devices with their start and end apart: 1, of which 1 were waited for; matrix products, arithmetic and copies ran while one was open for 0% of the time, Pallas kernels for 2%

profile of v5, /device:TPU:2, one launch (start us, length us, event | category | flops | bytes accessed | tf_op | source)
XLA Modules:
  0.0 120.4 jit_solution(13047802596429169810)
XLA Ops:
  0.0 3.9 %shard_map.100 = bf16[128,64,128]{2,1,0:T(8,128)(2,1)S(1)} custom-call(bf16[62,62,128]{2,1,0:T(8,128)(2,1)} %pair_ref.1, s32[62,62]{1,0:T(8,128)} %mask_hbm.1, f32[1,128]{1,0:T(1,128)} %bitcast.4, bf16[128,512]{1,0:T(8,128)(2,1)} %weight_hbm.1), custom_call_target="tpu_custom_call" | custom-call | tf_op jit(solution)/shard_map/pallas_call | solution.py:104
  3.9 68.2 %all_to_all.10.in_ref = bf16[128,64,128]{2,1,0:T(8,128)(2,1)S(1)} all-to-all(bf16[128,64,128]{2,1,0:T(8,128)(2,1)S(1)} %shard_map.100), channel_id=1, replica_groups=mesh['row'=16,'chip'=8,'core'=2] {'row','chip'}, dimensions={0} | all-to-all | bytes 4194304 | tf_op jit(solution)/shard_map/all_to_all | solution.py:299
  72.1 0.0 copy-start
  72.1 0.0 copy-start.3
  72.1 0.0 copy-start.5
  72.1 1.4 %shard_map.102 = bf16[128,32,128]{2,1,0:T(8,128)(2,1)S(1)} custom-call(s32[1]{0:T(128)S(6)} %sub.3.parity_ref, bf16[128,64,128]{2,1,0:T(8,128)(2,1)S(1)} %all_to_all.10.in_ref), custom_call_target="tpu_custom_call" | custom-call | tf_op jit(solution)/shard_map/pallas_call | solution.py:159
  73.5 0.1 collective-permute-start
  73.6 0.0 copy-done
  73.6 0.0 copy-done.3
  73.6 0.0 copy-done.5
  73.6 2.4 %shard_map.101 = (bf16[128,32,128]{2,1,0:T(8,128)(2,1)S(1)}, bf16[4096,128]{1,0:T(8,128)(2,1)S(1)}, f32[4096,128]{1,0:T(8,128)S(1)}) custom-call(s32[1]{0:T(128)} %bitcast.1.parity_ref, bf16[128,64,128]{2,1,0:T(8,128)(2,1)S(1)} %all_to_all.10.in_ref, bf16[62,62,128]{2,1,0:T(8,128)(2,1)S(1)} %copy-done, f32[1,128]{1,0:T(1,128)S(1)} %bitcast.5, ...), custom_call_target="tpu_custom_call" | custom-call | tf_op jit(solution)/shard_map/pallas_call | solution.py:187
  76.1 0.2 collective-permute-done
  76.2 0.0 copy-start.1
  76.2 0.0 copy-start.2
  76.3 0.0 copy-start.4
  76.3 0.0 copy-start.6
  76.3 0.0 copy-start.7
  76.3 0.3 add_convert_fusion
  76.6 37.7 %all_to_all.11.in_ref = bf16[128,32,128]{2,1,0:T(8,128)(2,1)S(1)} all-to-all(bf16[128,32,128]{2,1,0:T(8,128)(2,1)S(1)} %add_convert_fusion), channel_id=1, replica_groups=mesh['row'=16,'chip'=8,'core'=2] {'row','chip'}, dimensions={0} | all-to-all | bytes 2097152 | tf_op jit(solution)/shard_map/all_to_all | solution.py:304
  114.2 0.0 copy-done.1
  114.2 0.0 copy-done.2
  114.2 0.0 copy-done.4
  114.2 0.0 copy-done.6
  114.3 0.0 copy-done.7
  114.3 6.0 %shard_map.103 = bf16[62,62,128]{2,1,0:T(8,128)(2,1)} custom-call(bf16[4096,128]{1,0:T(8,128)(2,1)S(1)} %get-tuple-element.20.rows_ref, f32[4096,128]{1,0:T(8,128)S(1)} %get-tuple-element.21.gate_ref, bf16[128,32,128]{2,1,0:T(8,128)(2,1)S(1)} %all_to_all.11.in_ref, f32[1,128]{1,0:T(1,128)S(1)} %bitcast.6, bf16[128,128]{1,0:T(8,128)(2,1)S(1)} %copy-done.4, ...), custom_call_target="tpu_custom_call" | custom-call | tf_op jit(solution)/shard_map/pallas_call | solution.py:260
Async XLA Ops:
  72.1 1.5 %copy-start = (bf16[62,62,128]{2,1,0:T(8,128)(2,1)S(1)}, bf16[62,62,128]{2,1,0:T(8,128)(2,1)}, u32[]{:S(2)}) copy-start(bf16[62,62,128]{2,1,0:T(8,128)(2,1)} %pair_ref.1) | copy-start | bytes 2952196
  72.1 1.5 %copy-start.3 = (bf16[128,128]{1,0:T(8,128)(2,1)S(1)}, bf16[128,128]{1,0:T(8,128)(2,1)}, u32[]{:S(2)}) copy-start(bf16[128,128]{1,0:T(8,128)(2,1)} %gate_ref.1) | copy-start | bytes 98308
  72.1 1.5 %copy-start.5 = (f32[128]{0:T(128)S(1)}, f32[128]{0:T(128)}, u32[]{:S(2)}) copy-start(f32[128]{0:T(128)} %param.12) | copy-start | bytes 1540
  73.5 2.7 %collective-permute-start = (bf16[128,32,128]{2,1,0:T(8,128)(2,1)S(1)}, bf16[128,32,128]{2,1,0:T(8,128)(2,1)S(1)}, u32[]{:S(2)}, u32[]{:S(2)}) collective-permute-start(bf16[128,32,128]{2,1,0:T(8,128)(2,1)S(1)} %shard_map.102), channel_id=1, source_target_pairs={{0,1},{1,0},{2,3},{3,2},{4,5},{5,4},{6,7},{7,6},{8,9},{9,8},{10,11... | collective-permute-start | bytes 3145736 | tf_op jit(solution)/shard_map/ppermute | solution.py:300
  76.2 38.0 %copy-start.1 = (bf16[128,1024]{1,0:T(8,128)(2,1)S(1)}, bf16[128,1024]{1,0:T(8,128)(2,1)}, u32[]{:S(2)}) copy-start(bf16[128,1024]{1,0:T(8,128)(2,1)} %tr_in_ref.1) | copy-start | bytes 786436
  76.2 38.0 %copy-start.2 = (bf16[512,128]{1,0:T(8,128)(2,1)S(1)}, bf16[512,128]{1,0:T(8,128)(2,1)}, u32[]{:S(2)}) copy-start(bf16[512,128]{1,0:T(8,128)(2,1)} %tr_out_ref.1) | copy-start | bytes 393220
  76.3 38.0 %copy-start.4 = (bf16[128,128]{1,0:T(8,128)(2,1)S(1)}, bf16[128,128]{1,0:T(8,128)(2,1)}, u32[]{:S(2)}) copy-start(bf16[128,128]{1,0:T(8,128)(2,1)} %out_weight_ref.1) | copy-start | bytes 98308
  76.3 38.0 %copy-start.6 = (f32[128]{0:T(128)S(1)}, f32[128]{0:T(128)}, u32[]{:S(2)}) copy-start(f32[128]{0:T(128)} %param.15) | copy-start | bytes 1540
  76.3 38.0 %copy-start.7 = (f32[128]{0:T(128)S(1)}, f32[128]{0:T(128)}, u32[]{:S(2)}) copy-start(f32[128]{0:T(128)} %param.17) | copy-start | bytes 1540
